TPU v7x, 32 devices: a whole 2x2x4 slice. The times are simulated.
32 devices in a mesh: dp: 16 (over z, y, core), tensor: 2 (over x).
Axes of the slice: x: 2, y: 2, z: 4, core: 2. Of those that a mesh axis runs over, the one named last changes fastest.
Arguments:
- block_input: bfloat16 [16384, 1024], P(('dp', 'tensor')), may hold values from -6 to 6
- segment_ids: int32 [16384], P('dp'), may hold values from 0 to 2, as said below
- ln1_gain: float32 [1024], replicated, may hold values from 0.1 to 1.9
- ln1_bias: float32 [1024], replicated, may hold values from -4 to 4
- w_query: bfloat16 [1024, 1024], P('dp', 'tensor'), may hold values from -0.1875 to 0.1875
- w_key: bfloat16 [1024, 1024], P('dp', 'tensor'), may hold values from -0.1875 to 0.1875
- w_value: bfloat16 [1024, 1024], P('dp', 'tensor'), may hold values from -0.1875 to 0.1875
- b_query: float32 [1024], replicated, may hold values from -6 to 6
- b_value: float32 [1024], replicated, may hold values from -6 to 6
- w_out: bfloat16 [1024, 1024], P('dp', 'tensor'), may hold values from -1 to 1
- b_out: float32 [1024], replicated, may hold values from -4 to 4
- ln2_gain: float32 [1024], replicated, may hold values from 0.1 to 1.9
- ln2_bias: float32 [1024], replicated, may hold values from -4 to 4
- w_up: bfloat16 [1024, 4096], P('dp', 'tensor'), may hold values from -0.1875 to 0.1875
- b_up: float32 [4096], replicated, may hold values from -6 to 6
- w_down: bfloat16 [1024, 4096], P('dp', 'tensor'), may hold values from -0.125 to 0.125
- b_down: float32 [1024], replicated, may hold values from -4 to 4
- out_grad: bfloat16 [16384, 1024], P(('dp', 'tensor')), may hold values from -6 to 6
Outputs:
- block_output: bfloat16 [16384, 1024], P(('dp', 'tensor'))
- grad_input: bfloat16 [16384, 1024], P(('dp', 'tensor'))
- grad_ln1_gain: float32 [1024], replicated
- grad_ln1_bias: float32 [1024], replicated
- grad_w_query: float32 [1024, 1024], P('dp', 'tensor')
- grad_w_key: float32 [1024, 1024], P('dp', 'tensor')
- grad_w_value: float32 [1024, 1024], P('dp', 'tensor')
- grad_b_query: float32 [1024], replicated
- grad_b_value: float32 [1024], replicated
- grad_w_out: float32 [1024, 1024], P('dp', 'tensor')
- grad_b_out: float32 [1024], replicated
- grad_ln2_gain: float32 [1024], replicated
- grad_ln2_bias: float32 [1024], replicated
- grad_w_up: float32 [1024, 4096], P('dp', 'tensor')
- grad_b_up: float32 [4096], replicated
- grad_w_down: float32 [1024, 4096], P('dp', 'tensor')
- grad_b_down: float32 [1024], replicated
Inputs may be any that keep to these rules, and one draw needn't show every extreme that they name: `segment_ids`: within each data group of 1024 consecutive tokens the ids are 0, 1 and 2, each present, never falling; the block's attention never reaches across data groups.
All inputs are finite; a program needn't handle non-finite values.
Results may differ from a plain program's by a relative error of at most 0.018.
Values may be sent and summed in bfloat16 or wider, within the bound.
No kernel may reach another device: no remote copies, remote signals or barrier semaphores. Data moves between devices by JAX's collectives and lax.ppermute only.
A program may use at most 192 MiB of HBM per device.

v0:
```python
import jax
import jax.numpy as jnp
from jax import lax
from jax.sharding import PartitionSpec as P

HEAD_DIM = 64


def normalize(values, gain_vec, bias_vec):
    center = values - jnp.mean(values, axis=-1, keepdims=True)
    spread = jnp.mean(center * center, axis=-1, keepdims=True)
    inverse = lax.rsqrt(spread + 1e-05)
    scaled = center * inverse
    return (scaled * gain_vec + bias_vec, scaled, inverse)


def norm_back(grad_in, scaled, inverse, gain_vec):
    local_grad = grad_in * gain_vec
    return inverse * (
        local_grad
        - jnp.mean(local_grad, axis=-1, keepdims=True)
        - scaled * jnp.mean(local_grad * scaled, axis=-1, keepdims=True)
    )


def gelu_tanh(values):
    return (
        0.5
        * values
        * (1.0 + jnp.tanh(0.7978845608028654 * (values + 0.044715 * values * values * values)))
    )


def split_heads(matrix):
    return matrix.reshape(matrix.shape[0], -1, HEAD_DIM).transpose(1, 0, 2)


def join_heads(stacked):
    return stacked.transpose(1, 0, 2).reshape(stacked.shape[1], -1)


def contract_rows(left_mat, right_mat):
    return lax.dot_general(
        left_mat, right_mat, (((0,), (0,)), ((), ())), preferred_element_type=jnp.float32
    )


def contract_cols(left_mat, right_mat):
    return lax.dot_general(
        left_mat, right_mat, (((1,), (1,)), ((), ())), preferred_element_type=jnp.float32
    )


def block_mask(group_ids, first_row, block_rows):
    group_len = group_ids.shape[0]
    row_places = first_row + jnp.arange(block_rows)
    col_places = jnp.arange(group_len)
    row_ids = lax.dynamic_slice_in_dim(group_ids, first_row, block_rows)
    return (row_ids[:, None] == group_ids[None, :]) & (row_places[:, None] >= col_places[None, :])


def block_scores(query_block, key_heads, allowed):
    scores = jnp.einsum("hqd,hkd->hqk", query_block, key_heads, preferred_element_type=jnp.float32)
    scores = scores * HEAD_DIM ** (-0.5)
    return jnp.where(allowed[None], scores, -1e30)


def per_device(
    block_input,
    segment_ids,
    ln1_gain,
    ln1_bias,
    w_query,
    w_key,
    w_value,
    b_query,
    b_value,
    w_out,
    b_out,
    ln2_gain,
    ln2_bias,
    w_up,
    b_up,
    w_down,
    b_down,
    out_grad,
):
    group_len = segment_ids.shape[0]
    block_rows = min(512, group_len)
    block_count = group_len // block_rows
    tensor_rank = lax.axis_index("tensor")
    head_width = w_query.shape[1]
    unit_width = w_up.shape[1]
    head_first = tensor_rank * head_width
    unit_first = tensor_rank * unit_width
    weights = (
        lax.all_gather(w_query, "dp", axis=0, tiled=True),
        lax.all_gather(w_key, "dp", axis=0, tiled=True),
        lax.all_gather(w_value, "dp", axis=0, tiled=True),
        lax.all_gather(w_out, "dp", axis=0, tiled=True),
        lax.all_gather(w_up, "dp", axis=0, tiled=True),
        lax.all_gather(w_down, "dp", axis=0, tiled=True),
    )
    full_query, full_key, full_value, full_out, full_up, full_down = weights
    bias_query = lax.dynamic_slice_in_dim(b_query, head_first, head_width)
    bias_value = lax.dynamic_slice_in_dim(b_value, head_first, head_width)
    bias_up = lax.dynamic_slice_in_dim(b_up, unit_first, unit_width)
    rows_in = block_input.astype(jnp.float32)
    normed, scaled_one, inverse_one = normalize(rows_in, ln1_gain, ln1_bias)
    group_normed = lax.all_gather(normed.astype(jnp.bfloat16), "tensor", axis=0, tiled=True)
    queries = (
        jnp.dot(group_normed, full_query, preferred_element_type=jnp.float32) + bias_query
    ).astype(jnp.bfloat16)
    key_rows = jnp.dot(group_normed, full_key, preferred_element_type=jnp.float32).astype(
        jnp.bfloat16
    )
    value_rows = (
        jnp.dot(group_normed, full_value, preferred_element_type=jnp.float32) + bias_value
    ).astype(jnp.bfloat16)
    query_heads = split_heads(queries)
    key_heads = split_heads(key_rows)
    value_heads = split_heads(value_rows)
    local_heads = query_heads.shape[0]

    def forward_block(block_index):
        first_row = block_index * block_rows
        query_block = lax.dynamic_slice_in_dim(query_heads, first_row, block_rows, 1)
        scores = block_scores(
            query_block, key_heads, block_mask(segment_ids, first_row, block_rows)
        )
        row_peak = jnp.max(scores, axis=-1, keepdims=True)
        exponent = jnp.exp(scores - row_peak)
        row_total = jnp.sum(exponent, axis=-1, keepdims=True)
        attn_probs = (exponent / row_total).astype(jnp.bfloat16)
        mixed_block = jnp.einsum(
            "hqk,hkd->hqd", attn_probs, value_heads, preferred_element_type=jnp.float32
        )
        return (mixed_block.astype(jnp.bfloat16), row_peak[..., 0] + jnp.log(row_total[..., 0]))

    mixed_blocks, total_blocks = lax.map(forward_block, jnp.arange(block_count))
    mixed_heads = mixed_blocks.transpose(1, 0, 2, 3).reshape(query_heads.shape)
    log_total = total_blocks.transpose(1, 0, 2).reshape(local_heads, group_len)
    mixed_rows = join_heads(mixed_heads)
    attended = lax.psum_scatter(
        contract_cols(mixed_rows, full_out), "tensor", scatter_dimension=0, tiled=True
    )
    hidden = rows_in + attended + b_out
    normed_two, scaled_two, inverse_two = normalize(hidden, ln2_gain, ln2_bias)
    group_two = lax.all_gather(normed_two.astype(jnp.bfloat16), "tensor", axis=0, tiled=True)
    pre_active = jnp.dot(group_two, full_up, preferred_element_type=jnp.float32) + bias_up
    active = gelu_tanh(pre_active).astype(jnp.bfloat16)
    output = (
        hidden
        + lax.psum_scatter(
            contract_cols(active, full_down).astype(jnp.bfloat16),
            "tensor",
            scatter_dimension=0,
            tiled=True,
        ).astype(jnp.float32)
        + b_down
    )
    back_weights = (
        lax.all_gather(w_query, "dp", axis=0, tiled=True),
        lax.all_gather(w_key, "dp", axis=0, tiled=True),
        lax.all_gather(w_value, "dp", axis=0, tiled=True),
        lax.all_gather(w_out, "dp", axis=0, tiled=True),
        lax.all_gather(w_up, "dp", axis=0, tiled=True),
        lax.all_gather(w_down, "dp", axis=0, tiled=True),
    )
    back_query, back_key, back_value, back_out, back_up, back_down = back_weights
    grad_rows = out_grad.astype(jnp.float32)
    group_grad = lax.all_gather(out_grad, "tensor", axis=0, tiled=True)
    grad_active = jnp.dot(group_grad, back_down, preferred_element_type=jnp.float32)
    gelu_pull = jax.vjp(gelu_tanh, pre_active)[1]
    grad_pre = gelu_pull(grad_active)[0].astype(jnp.bfloat16)
    grad_w_down_part = contract_rows(group_grad, active)
    grad_w_up_part = contract_rows(group_two, grad_pre)
    grad_normed_two = lax.psum_scatter(
        contract_cols(grad_pre, back_up).astype(jnp.bfloat16),
        "tensor",
        scatter_dimension=0,
        tiled=True,
    ).astype(jnp.float32)
    grad_hidden = grad_rows + norm_back(grad_normed_two, scaled_two, inverse_two, ln2_gain)
    group_attn_grad = lax.all_gather(grad_hidden.astype(jnp.bfloat16), "tensor", axis=0, tiled=True)
    grad_w_out_part = contract_rows(group_attn_grad, mixed_rows)
    grad_mixed = jnp.dot(group_attn_grad, back_out, preferred_element_type=jnp.float32).astype(
        jnp.bfloat16
    )
    grad_heads = split_heads(grad_mixed)

    def backward_block(carried, block_index):
        key_sum, value_sum = carried
        first_row = block_index * block_rows
        query_block = lax.dynamic_slice_in_dim(query_heads, first_row, block_rows, 1)
        grad_block = lax.dynamic_slice_in_dim(grad_heads, first_row, block_rows, 1)
        total_block = lax.dynamic_slice_in_dim(log_total, first_row, block_rows, 1)
        scores = block_scores(
            query_block, key_heads, block_mask(segment_ids, first_row, block_rows)
        )
        attn_probs = jnp.exp(scores - total_block[..., None])
        value_sum = value_sum + jnp.einsum(
            "hqk,hqd->hkd",
            attn_probs.astype(jnp.bfloat16),
            grad_block,
            preferred_element_type=jnp.float32,
        )
        grad_probs = jnp.einsum(
            "hqd,hkd->hqk", grad_block, value_heads, preferred_element_type=jnp.float32
        )
        inner_sum = jnp.sum(attn_probs * grad_probs, axis=-1, keepdims=True)
        grad_scores = (attn_probs * (grad_probs - inner_sum)).astype(jnp.bfloat16)
        grad_query = jnp.einsum(
            "hqk,hkd->hqd", grad_scores, key_heads, preferred_element_type=jnp.float32
        ) * HEAD_DIM ** (-0.5)
        key_sum = key_sum + jnp.einsum(
            "hqk,hqd->hkd", grad_scores, query_block, preferred_element_type=jnp.float32
        ) * HEAD_DIM ** (-0.5)
        return ((key_sum, value_sum), grad_query.astype(jnp.bfloat16))

    zero_heads = jnp.zeros(key_heads.shape, jnp.float32)
    (key_sum, value_sum), query_blocks = lax.scan(
        backward_block, (zero_heads, zero_heads), jnp.arange(block_count)
    )
    grad_queries = join_heads(query_blocks.transpose(1, 0, 2, 3).reshape(query_heads.shape))
    grad_keys = join_heads(key_sum).astype(jnp.bfloat16)
    grad_values = join_heads(value_sum).astype(jnp.bfloat16)
    grad_w_query_part = contract_rows(group_normed, grad_queries)
    grad_w_key_part = contract_rows(group_normed, grad_keys)
    grad_w_value_part = contract_rows(group_normed, grad_values)
    part_query = contract_cols(grad_queries, back_query)
    part_key = contract_cols(grad_keys, back_key)
    part_value = contract_cols(grad_values, back_value)
    grad_normed = lax.psum_scatter(
        (part_query + part_key + part_value).astype(jnp.bfloat16),
        "tensor",
        scatter_dimension=0,
        tiled=True,
    ).astype(jnp.float32)
    grad_input = grad_hidden + norm_back(grad_normed, scaled_one, inverse_one, ln1_gain)
    weight_sums = (
        lax.psum_scatter(
            grad_w_query_part.astype(jnp.bfloat16), "dp", scatter_dimension=0, tiled=True
        ).astype(jnp.float32),
        lax.psum_scatter(
            grad_w_key_part.astype(jnp.bfloat16), "dp", scatter_dimension=0, tiled=True
        ).astype(jnp.float32),
        lax.psum_scatter(
            grad_w_value_part.astype(jnp.bfloat16), "dp", scatter_dimension=0, tiled=True
        ).astype(jnp.float32),
        lax.psum_scatter(
            grad_w_out_part.astype(jnp.bfloat16), "dp", scatter_dimension=0, tiled=True
        ).astype(jnp.float32),
        lax.psum_scatter(
            grad_w_up_part.astype(jnp.bfloat16), "dp", scatter_dimension=0, tiled=True
        ).astype(jnp.float32),
        lax.psum_scatter(
            grad_w_down_part.astype(jnp.bfloat16), "dp", scatter_dimension=0, tiled=True
        ).astype(jnp.float32),
    )
    query_bias_full = lax.dynamic_update_slice_in_dim(
        jnp.zeros(b_query.shape, jnp.float32),
        jnp.sum(grad_queries.astype(jnp.float32), axis=0),
        head_first,
        0,
    )
    value_bias_full = lax.dynamic_update_slice_in_dim(
        jnp.zeros(b_value.shape, jnp.float32),
        jnp.sum(grad_values.astype(jnp.float32), axis=0),
        head_first,
        0,
    )
    up_bias_full = lax.dynamic_update_slice_in_dim(
        jnp.zeros(b_up.shape, jnp.float32),
        jnp.sum(grad_pre.astype(jnp.float32), axis=0),
        unit_first,
        0,
    )
    small_sums = lax.psum(
        (
            jnp.sum(grad_normed * scaled_one, axis=0),
            jnp.sum(grad_normed, axis=0),
            query_bias_full,
            value_bias_full,
            jnp.sum(grad_hidden, axis=0),
            jnp.sum(grad_normed_two * scaled_two, axis=0),
            jnp.sum(grad_normed_two, axis=0),
            up_bias_full,
            jnp.sum(grad_rows, axis=0),
        ),
        ("dp", "tensor"),
    )
    return (
        output.astype(jnp.bfloat16),
        grad_input.astype(jnp.bfloat16),
        small_sums[0],
        small_sums[1],
        weight_sums[0],
        weight_sums[1],
        weight_sums[2],
        small_sums[2],
        small_sums[3],
        weight_sums[3],
        small_sums[4],
        small_sums[5],
        small_sums[6],
        weight_sums[4],
        small_sums[7],
        weight_sums[5],
        small_sums[8],
    )


def solution(mesh):
    return jax.shard_map(
        per_device,
        mesh=mesh,
        in_specs=(
            P(("dp", "tensor"), None),
            P("dp"),
            P(),
            P(),
            P("dp", "tensor"),
            P("dp", "tensor"),
            P("dp", "tensor"),
            P(),
            P(),
            P("dp", "tensor"),
            P(),
            P(),
            P(),
            P("dp", "tensor"),
            P(),
            P("dp", "tensor"),
            P(),
            P(("dp", "tensor"), None),
        ),
        out_specs=(
            P(("dp", "tensor"), None),
            P(("dp", "tensor"), None),
            P(),
            P(),
            P("dp", "tensor"),
            P("dp", "tensor"),
            P("dp", "tensor"),
            P(),
            P(),
            P("dp", "tensor"),
            P(),
            P(),
            P(),
            P("dp", "tensor"),
            P(),
            P("dp", "tensor"),
            P(),
        ),
        check_vma=False,
    )
```

profile of v0, /device:TPU:10, one launch (start us, length us, event | category | flops | bytes accessed | tf_op | source)
XLA Modules:
  0.0 1040.6 jit_solution(12398054789102264738)
XLA Ops:
  15.3 33.1 %all-gather.15.cloned.1.call-done = bf16[1024,512]{1,0:T(8,128)(2,1)} async-done(((bf16[64,512]{1,0:T(8,128)(2,1)}), bf16[1024,512]{1,0:T(8,128)(2,1)}) %all-gather.15.cloned.1.call-update) | async-done | bytes 1048592 | tf_op jit(solution)/shard_map/all_gather | solution.py:98
  48.4 34.2 %all-gather.11.cloned.1.call-done = bf16[1024,1024]{1,0:T(8,128)(2,1)} async-done(((bf16[512,1024]{1,0:T(8,128)(2,1)}), bf16[1024,1024]{1,0:T(8,128)(2,1)}) %all-gather.11.cloned.1.call-update) | async-done | bytes 2097168 | tf_op jit(solution)/shard_map/all_gather | solution.py:110
  85.8 36.9 %all-gather.17.cloned.1.call-done = bf16[1024,512]{1,0:T(8,128)(2,1)} async-done(((bf16[64,512]{1,0:T(8,128)(2,1)}), bf16[1024,512]{1,0:T(8,128)(2,1)}) %all-gather.17.cloned.1.call-update) | async-done | bytes 1048592 | tf_op jit(solution)/shard_map/all_gather | solution.py:99
  122.7 4.1 add_convert_fusion.3
  126.8 34.8 %all-gather.13.cloned.1.call-done = bf16[1024,512]{1,0:T(8,128)(2,1)} async-done(((bf16[64,512]{1,0:T(8,128)(2,1)}), bf16[1024,512]{1,0:T(8,128)(2,1)}) %all-gather.13.cloned.1.call-update) | async-done | bytes 1048592 | tf_op jit(solution)/shard_map/all_gather | solution.py:97
  161.6 4.1 add_convert_fusion.4
  165.8 32.6 %while.27 = (s32[]{:T(128)}, bf16[2,8,512,64]{2,3,1,0:T(8,128)(2,1)S(1)}, f32[2,8,512]{2,1,0:T(8,128)S(1)}, s32[2]{0:T(128)S(1)}, s32[1024]{0:T(1024)S(1)}, /*in...) while((s32[]{:T(128)}, ...), condition=%wide.region_5.6_spmd, body=%wide.region_2.5_spmd.sunk | while | flops 1125904896 | bytes 55720136 | solution.py:140
  168.0 4.1 fusion.129
  172.1 4.2 fusion.130
  176.3 5.9 fusion.131
  184.2 4.1 fusion.129
  188.3 4.2 fusion.130
  192.5 5.9 fusion.131
  200.5 4.5 fusion.63
  205.8 52.6 %reduce-scatter.13.cloned.1.call-done = f32[512,1024]{1,0:T(8,128)} async-done(((f32[1024,1024]{1,0:T(8,128)}), f32[512,1024]{1,0:T(8,128)}) %reduce-scatter.13.cloned.1.call-update) | async-done | bytes 2097168 | tf_op jit(solution)/shard_map/reduce_scatter | solution.py:144
  264.4 48.1 %all-gather.23.cloned.1.call-done = bf16[1024,2048]{1,0:T(8,128)(2,1)} async-done(((bf16[64,2048]{1,0:T(8,128)(2,1)}), bf16[1024,2048]{1,0:T(8,128)(2,1)}) %all-gather.23.cloned.1.call-update) | async-done | bytes 4194320 | tf_op jit(solution)/shard_map/all_gather | solution.py:101
  312.5 32.9 %all-gather.21.cloned.1.call-done = bf16[1024,1024]{1,0:T(8,128)(2,1)} async-done(((bf16[512,1024]{1,0:T(8,128)(2,1)}), bf16[1024,1024]{1,0:T(8,128)(2,1)}) %all-gather.21.cloned.1.call-update) | async-done | bytes 2097168 | tf_op jit(solution)/shard_map/all_gather | solution.py:149
  345.4 10.8 %fusion.64 = f32[1024,2048]{1,0:T(8,128)} fusion(bf16[1024,1024]{1,0:T(8,128)(2,1)} %all-gather.21.cloned.1.call-done, bf16[1024,2048]{1,0:T(8,128)(2,1)} %all-gather.23.cloned.1.call-done), kind=kOutput, calls=%fused_computation.119 | convolution fusion | flops 4294967296 | bytes 14680064 | tf_op jit(solution)/shard_map/dot_general | solution.py:150
  356.2 23.9 %all-gather.27.cloned.1.call-done = bf16[1024,1024]{1,0:T(8,128)(2,1)} async-done(((bf16[512,1024]{1,0:T(8,128)(2,1)}), bf16[1024,1024]{1,0:T(8,128)(2,1)}) %all-gather.27.cloned.1.call-update) | async-done | bytes 2097168 | tf_op jit(solution)/shard_map/all_gather | solution.py:172
  380.2 53.8 %all-gather.25.cloned.1.call-done = bf16[1024,2048]{1,0:T(8,128)(2,1)} async-done(((bf16[64,2048]{1,0:T(8,128)(2,1)}), bf16[1024,2048]{1,0:T(8,128)(2,1)}) %all-gather.25.cloned.1.call-update) | async-done | bytes 4194320 | tf_op jit(solution)/shard_map/all_gather | solution.py:102
  433.9 15.0 %convert_reduce_fusion = (f32[2048]{0:T(1024)}, bf16[1024,2048]{1,0:T(8,128)(2,1)S(1)}) fusion(f32[1024,2048]{1,0:T(8,128)} %fusion.64, f32[2048]{0:T(1024)S(1)} %dynamic_slice.36, bf16[1024,1024]{1,0:T(8,128)(2,1)} %all-gather.27.cloned.1.call-done, bf16[1024,2048]{1,0:T(8,128)(2,1)} %all-gather.25.cloned.1.call-done), kind=kOutput, calls=%fused_computation.52 | convolution fusion | flops 4351588352 | bytes 18890752 | tf_op jit(solution)/shard_map/dot_general | solution.py:173
  450.9 5.7 convolution_convert_fusion.1
  457.2 11.3 %convolution_convert_fusion.2 = bf16[1024,1024]{1,0:T(8,128)(2,1)} fusion(bf16[1024,2048]{1,0:T(8,128)(2,1)} %all-gather.25.cloned.1.call-done, f32[1024,2048]{1,0:T(8,128)} %fusion.64, f32[2048]{0:T(1024)S(1)} %dynamic_slice.36), kind=kOutput, calls=%fused_computation.101 | convolution fusion | flops 4316987392 | bytes 14688256 | tf_op jit(solution)/shard_map/dot_general | solution.py:49
  468.6 17.6 %reduce-scatter.17.cloned.1.call-done = bf16[512,1024]{1,0:T(8,128)(2,1)} async-done(((bf16[1024,1024]{1,0:T(8,128)(2,1)}), bf16[512,1024]{1,0:T(8,128)(2,1)}) %reduce-scatter.17.cloned.1.call-update) | async-done | bytes 1048592 | tf_op jit(solution)/shard_map/reduce_scatter | solution.py:178
  489.0 31.2 %reduce-scatter.15.cloned.1.call-done = bf16[512,1024]{1,0:T(8,128)(2,1)} async-done(((bf16[1024,1024]{1,0:T(8,128)(2,1)}), bf16[512,1024]{1,0:T(8,128)(2,1)}) %reduce-scatter.15.cloned.1.call-update) | async-done | bytes 1048592 | tf_op jit(solution)/shard_map/reduce_scatter | solution.py:154
  520.2 4.1 fusion.60
  527.6 11.8 %convert_bitcast_fusion = bf16[1024,2048]{0,1:T(8,128)(2,1)} fusion(bf16[1024,1024]{1,0:T(8,128)(2,1)S(1)} %copy-done.44, f32[1024,2048]{1,0:T(8,128)} %fusion.64, f32[2048]{0:T(1024)S(1)} %dynamic_slice.36), kind=kOutput, calls=%fused_computation.54 | convolution fusion | flops 4318035968 | bytes 14688256 | tf_op jit(solution)/shard_map/dot_general | solution.py:43
  539.4 6.5 copy.42
  547.5 8.3 convolution_convert_fusion
  555.9 4.2 all-gather.29.cloned.1.call-done
  560.1 3.9 convolution_convert_fusion.3
  564.0 3.9 convolution_convert_fusion.7
  569.0 90.6 %while.28 = (s32[]{:T(128)}, f32[8,1024,64]{1,2,0:T(8,128)}, f32[8,1024,64]{1,2,0:T(8,128)}, bf16[2,8,512,64]{2,3,1,0:T(8,128)(2,1)}, s32[2]{0:T(128)S(1)}, /*in...) while((s32[]{:T(128)}, f32[8,1024,64]{1,2,0:T(8,128)}, ...), condition=%wide.region_15.16_spmd.clone, body=%wide.region_13.15_spmd.clone.sunk | while | flops 2726818304 | bytes 204306928 | solution.py:222
  572.5 3.9 fusion.141
  576.4 11.5 %multiply_reduce_fusion.3 = (f32[8,512]{1,0:T(8,128)}, f32[8,512,1024]{2,1,0:T(8,128)}) fusion(f32[8,512,1024]{2,1,0:T(8,128)S(1)} %fusion.141, f32[8,512]{1,0:T(8,128)} %constant_dynamic-slice_fusion.2, bf16[8,1024,64]{1,2,0:T(8,128)(2,1)S(1)} %get-tuple-element.479, bf16[8,1024,64]{1,2,0:T(8,128)(2,1)} %get-tuple-element.478, s32[]{:T(128)S(6)} %select_n.57, ...), kind=kOutput, calls=%fused_computation.19.clone.1 | convolution fusion | flops 557838336 | bytes 35684356 | tf_op jit(solution)/shard_map/while/body/eval_jaxpr/hqd,hkd->hqk/dot_general | solution.py:63
  587.9 9.8 multiply_convert_fusion.5
  597.7 8.9 select_add_fusion.5
  621.0 11.5 %multiply_reduce_fusion.3 = (f32[8,512]{1,0:T(8,128)}, f32[8,512,1024]{2,1,0:T(8,128)}) fusion(f32[8,512,1024]{2,1,0:T(8,128)S(1)} %fusion.141, f32[8,512]{1,0:T(8,128)} %constant_dynamic-slice_fusion.2, bf16[8,1024,64]{1,2,0:T(8,128)(2,1)S(1)} %get-tuple-element.479, bf16[8,1024,64]{1,2,0:T(8,128)(2,1)} %get-tuple-element.478, s32[]{:T(128)S(6)} %select_n.57, ...), kind=kOutput, calls=%fused_computation.19.clone.1 | convolution fusion | flops 557838336 | bytes 35684356 | tf_op jit(solution)/shard_map/while/body/eval_jaxpr/hqd,hkd->hqk/dot_general | solution.py:63
  632.4 9.5 multiply_convert_fusion.5
  641.9 9.9 select_add_fusion.5
  670.4 4.0 convolution_convert_fusion.4
  685.1 27.2 %reduce-scatter.29.cloned.1.call-done = bf16[64,2048]{1,0:T(8,128)(2,1)} async-done(((bf16[1024,2048]{1,0:T(8,128)(2,1)}), bf16[64,2048]{1,0:T(8,128)(2,1)}) %reduce-scatter.29.cloned.1.call-update) | async-done | bytes 262160 | tf_op jit(solution)/shard_map/reduce_scatter | solution.py:254
  714.0 59.0 %reduce-scatter.27.cloned.1.call-done = bf16[64,512]{1,0:T(8,128)(2,1)} async-done(((bf16[1024,512]{1,0:T(8,128)(2,1)}), bf16[64,512]{1,0:T(8,128)(2,1)}) %reduce-scatter.27.cloned.1.call-update) | async-done | bytes 65552 | tf_op jit(solution)/shard_map/reduce_scatter | solution.py:251
  774.6 58.4 %reduce-scatter.21.cloned.1.call-done = bf16[64,512]{1,0:T(8,128)(2,1)} async-done(((bf16[1024,512]{1,0:T(8,128)(2,1)}), bf16[64,512]{1,0:T(8,128)(2,1)}) %reduce-scatter.21.cloned.1.call-update) | async-done | bytes 65552 | tf_op jit(solution)/shard_map/reduce_scatter | solution.py:242
  834.5 58.8 %reduce-scatter.23.cloned.1.call-done = bf16[64,512]{1,0:T(8,128)(2,1)} async-done(((bf16[1024,512]{1,0:T(8,128)(2,1)}), bf16[64,512]{1,0:T(8,128)(2,1)}) %reduce-scatter.23.cloned.1.call-update) | async-done | bytes 65552 | tf_op jit(solution)/shard_map/reduce_scatter | solution.py:245
  894.8 58.6 %reduce-scatter.25.cloned.1.call-done = bf16[64,512]{1,0:T(8,128)(2,1)} async-done(((bf16[1024,512]{1,0:T(8,128)(2,1)}), bf16[64,512]{1,0:T(8,128)(2,1)}) %reduce-scatter.25.cloned.1.call-update) | async-done | bytes 65552 | tf_op jit(solution)/shard_map/reduce_scatter | solution.py:248
  954.9 30.8 %reduce-scatter.19.cloned.1.call-done = bf16[512,1024]{1,0:T(8,128)(2,1)} async-done(((bf16[1024,1024]{1,0:T(8,128)(2,1)}), bf16[512,1024]{1,0:T(8,128)(2,1)}) %reduce-scatter.19.cloned.1.call-update) | async-done | bytes 1048592 | tf_op jit(solution)/shard_map/reduce_scatter | solution.py:234
  988.0 42.3 %all-reduce = (f32[1024]{0:T(1024)}, f32[1024]{0:T(1024)}, f32[1024]{0:T(1024)}, f32[1024]{0:T(1024)}, f32[1024]{0:T(1024)}, /*index=5*/f32[1024]{0:T(1024)}, f32[1024]{0:T(1024)}, f32[4096]{0:T(1024)}, f32[1024]{0:T(1024)}) all-reduce(f32[1024]{0:T(1024)S(1)} %get-tuple-element.213, ...), channel_id=1, replica_groups=mesh['dp'=16,'tensor'=2] {'dp','tensor'}, use_global_device_ids=true, to_apply=%region_20.21 | all-reduce | flops 12288 | bytes 98304 | tf_op jit(solution)/shard_map/psum | solution.py:279
  (232 shorter events, 92.1 us)
Async XLA Ops:
  7.2 4.5 copy-start.4
  7.2 4.5 copy-start.24
  7.2 4.5 copy-start.34
  7.2 41.1 %all-gather.15.cloned.1.call-start = ((), (), s32[]{:S(2)}) async-start(), calls=%async_computation.12 | async-start | bytes 1114112 | tf_op jit(solution)/shard_map/all_gather | solution.py:98
  8.0 74.6 %all-gather.11.cloned.1.call-start = ((), (), s32[]{:S(2)}) async-start(), calls=%async_computation.10 | async-start | bytes 3145728 | tf_op jit(solution)/shard_map/all_gather | solution.py:110
  9.5 5.7 copy-start.38
  9.5 5.8 copy-start.39
  13.2 109.5 %all-gather.17.cloned.1.call-start = ((), (), s32[]{:S(2)}) async-start(), calls=%async_computation.13 | async-start | bytes 1114112 | tf_op jit(solution)/shard_map/all_gather | solution.py:99
  13.9 147.7 %all-gather.13.cloned.1.call-start = ((), (), s32[]{:S(2)}) async-start(), calls=%async_computation.11 | async-start | bytes 1114112 | tf_op jit(solution)/shard_map/all_gather | solution.py:97
  14.5 186.0 %all-gather.19.cloned.1.call-start = ((), (), s32[]{:S(2)}) async-start(), calls=%async_computation.14 | async-start | bytes 1114112 | tf_op jit(solution)/shard_map/all_gather | solution.py:100
  15.1 243.3 %reduce-scatter.13.cloned.1.call-start = ((), (), s32[]{:S(2)}) async-start(), calls=%async_computation.15 | async-start | bytes 6291456 | tf_op jit(solution)/shard_map/reduce_scatter | solution.py:144
  126.8 39.0 %copy-start.18 = (s32[1024]{0:T(1024)S(1)}, s32[1024]{0:T(1024)}, u32[]{:S(2)}) copy-start(s32[1024]{0:T(1024)} %param.23) | copy-start | bytes 12292
  198.6 6.4 copy-start.16
  205.0 53.4 %copy-start.37 = (f32[1024]{0:T(1024)S(1)}, f32[1024]{0:T(1024)}, u32[]{:S(2)}) copy-start(f32[1024]{0:T(1024)} %param.32) | copy-start | bytes 12292
  205.0 107.5 %all-gather.23.cloned.1.call-start = ((), (), s32[]{:S(2)}) async-start(), calls=%async_computation.17 | async-start | bytes 4456448 | tf_op jit(solution)/shard_map/all_gather | solution.py:101
  205.8 139.7 %all-gather.21.cloned.1.call-start = ((), (), s32[]{:S(2)}) async-start(), calls=%async_computation.16 | async-start | bytes 3145728 | tf_op jit(solution)/shard_map/all_gather | solution.py:149
  262.7 117.5 %all-gather.27.cloned.1.call-start = ((), (), s32[]{:S(2)}) async-start(), calls=%async_computation.20 | async-start | bytes 3145728 | tf_op jit(solution)/shard_map/all_gather | solution.py:172
  263.5 170.5 %all-gather.25.cloned.1.call-start = ((), (), s32[]{:S(2)}) async-start(), calls=%async_computation.18 | async-start | bytes 4456448 | tf_op jit(solution)/shard_map/all_gather | solution.py:102
  264.0 222.2 %reduce-scatter.17.cloned.1.call-start = ((), (), s32[]{:S(2)}) async-start(), calls=%async_computation.21 | async-start | bytes 3145728 | tf_op jit(solution)/shard_map/reduce_scatter | solution.py:178
  433.9 16.9 %copy-start.40 = (bf16[1024,2048]{1,0:T(8,128)(2,1)S(1)}, bf16[1024,2048]{1,0:T(8,128)(2,1)}, u32[]{:S(2)}) copy-start(bf16[1024,2048]{1,0:T(8,128)(2,1)} %all-gather.23.cloned.1.call-done) | copy-start | bytes 12582916
  456.7 63.5 %reduce-scatter.15.cloned.1.call-start = ((), (), s32[]{:S(2)}) async-start(), calls=%async_computation.19 | async-start | bytes 3145728 | tf_op jit(solution)/shard_map/reduce_scatter | solution.py:154
  468.5 51.6 %copy-start.33 = (f32[1024]{0:T(1024)S(1)}, f32[1024]{0:T(1024)}, u32[]{:S(2)}) copy-start(f32[1024]{0:T(1024)} %param.38) | copy-start | bytes 12292
  468.5 91.5 %all-gather.29.cloned.1.call-start = ((), (), s32[]{:S(2)}) async-start(), calls=%async_computation.22 | async-start | bytes 3145728 | tf_op jit(solution)/shard_map/all_gather | solution.py:185
  526.8 156.0 %reduce-scatter.31.cloned.1.call-start = ((), (), s32[]{:S(2)}) async-start(), calls=%async_computation.29 | async-start | bytes 4456448
  545.9 166.3 %reduce-scatter.29.cloned.1.call-start = ((), (), s32[]{:S(2)}) async-start(), calls=%async_computation.28 | async-start | bytes 4456448 | tf_op jit(solution)/shard_map/reduce_scatter | solution.py:254
  555.8 217.3 %reduce-scatter.27.cloned.1.call-start = ((), (), s32[]{:S(2)}) async-start(), calls=%async_computation.27 | async-start | bytes 1114112 | tf_op jit(solution)/shard_map/reduce_scatter | solution.py:251
  555.9 8.2 copy-start.46
  564.0 269.0 %reduce-scatter.21.cloned.1.call-start = ((), (), s32[]{:S(2)}) async-start(), calls=%async_computation.24 | async-start | bytes 1114112 | tf_op jit(solution)/shard_map/reduce_scatter | solution.py:242
  587.9 9.8 copy-start.6
  597.7 8.9 copy-start
  597.7 8.9 copy-start.11
  609.3 4.6 copy-start.20
  632.4 9.5 copy-start.6
  641.9 9.9 copy-start
  641.9 10.4 %copy-start.11 = (bf16[2,8,512,64]{2,3,1,0:T(8,128)(2,1)S(1)}, bf16[2,8,512,64]{2,3,1,0:T(8,128)(2,1)}, u32[]{:S(2)}) copy-start(bf16[2,8,512,64]{2,3,1,0:T(8,128)(2,1)} %get-tuple-element.460) | copy-start | bytes 3145732 | tf_op jit(solution)/shard_map/while
  655.0 4.6 copy-start.20
  663.9 229.4 %reduce-scatter.23.cloned.1.call-start = ((), (), s32[]{:S(2)}) async-start(), calls=%async_computation.25 | async-start | bytes 1114112 | tf_op jit(solution)/shard_map/reduce_scatter | solution.py:245
  668.6 284.9 %reduce-scatter.25.cloned.1.call-start = ((), (), s32[]{:S(2)}) async-start(), calls=%async_computation.26 | async-start | bytes 1114112 | tf_op jit(solution)/shard_map/reduce_scatter | solution.py:248
  674.4 311.3 %reduce-scatter.19.cloned.1.call-start = ((), (), s32[]{:S(2)}) async-start(), calls=%async_computation.23 | async-start | bytes 3145728 | tf_op jit(solution)/shard_map/reduce_scatter | solution.py:234
  682.0 303.6 %copy-start.5 = (bf16[512,1024]{1,0:T(8,128)(2,1)S(1)}, bf16[512,1024]{1,0:T(8,128)(2,1)}, u32[]{:S(2)}) copy-start(bf16[512,1024]{1,0:T(8,128)(2,1)} %param.22) | copy-start | bytes 3145732
  682.0 303.6 %copy-start.22 = (f32[512]{0:T(512)S(1)}, f32[512]{0:T(512)}, u32[]{:S(2)}) copy-start(f32[512]{0:T(512)} %copy-done.21) | copy-start | bytes 6148
  682.0 303.6 %copy-start.25 = (f32[1024]{0:T(1024)S(1)}, f32[1024]{0:T(1024)}, u32[]{:S(2)}) copy-start(f32[1024]{0:T(1024)} %param.24) | copy-start | bytes 12292
  682.0 303.6 %copy-start.27 = (f32[512]{0:T(512)S(1)}, f32[512]{0:T(512)}, u32[]{:S(2)}) copy-start(f32[512]{0:T(512)} %copy-done.26) | copy-start | bytes 6148
  685.0 302.9 %copy-start.28 = (f32[1024]{0:T(1024)S(1)}, f32[1024]{0:T(1024)}, u32[]{:S(2)}) copy-start(f32[1024]{0:T(1024)} %get-tuple-element.268) | copy-start | bytes 12292
  685.0 302.9 %copy-start.29 = (f32[1024]{0:T(1024)S(1)}, f32[1024]{0:T(1024)}, u32[]{:S(2)}) copy-start(f32[1024]{0:T(1024)} %get-tuple-element.279) | copy-start | bytes 12292
  685.0 302.9 %copy-start.30 = (f32[1024]{0:T(1024)S(1)}, f32[1024]{0:T(1024)}, u32[]{:S(2)}) copy-start(f32[1024]{0:T(1024)} %get-tuple-element.211) | copy-start | bytes 12292
  685.0 302.9 %copy-start.31 = (f32[1024]{0:T(1024)S(1)}, f32[1024]{0:T(1024)}, u32[]{:S(2)}) copy-start(f32[1024]{0:T(1024)} %get-tuple-element.217) | copy-start | bytes 12292
  685.0 345.3 %copy-start.8 = (f32[512,1024]{1,0:T(8,128)S(1)}, f32[512,1024]{1,0:T(8,128)}, u32[]{:S(2)}) copy-start(f32[512,1024]{1,0:T(8,128)} %copy-done.7) | copy-start | bytes 6291460
  (28 other events, 61.3 us)
Sparse Core Ops, SparseCore 0:
  10.2 38.0 all-gather.14
  50.5 32.0 all-gather.10
  84.8 37.8 all-gather.16
  124.7 36.8 all-gather.12
  163.6 36.8 all-gather.18
  205.1 53.2 reduce-scatter.12
  260.8 51.6 all-gather.22
  314.7 30.6 all-gather.20
  347.0 33.1 all-gather.26
  382.4 51.4 all-gather.24
  456.8 29.3 reduce-scatter.16
  488.3 31.8 reduce-scatter.14
  526.9 33.0 all-gather.28
  564.3 72.6 reduce-scatter.30
  640.6 71.5 reduce-scatter.28
  716.2 56.8 reduce-scatter.26
  776.5 56.4 reduce-scatter.20
  836.9 56.3 reduce-scatter.22
  896.9 56.4 reduce-scatter.24
  955.6 30.0 reduce-scatter.18
where the time goes:
time: 1050 us; the launch traced here: 1040 us
  waiting for transfers between devices  703 us (67%)
  matrix products  183 us (17%)
  other arithmetic  63.3 us (6%)
  blocking collectives  42.3 us (4%)
  local copies, waits for them, and re-layouts  28.8 us (3%)
  between operations  15.3 us (1%)
    reduce_scatter x1, waiting for transfers between devices, per_device(): lax.psum_scatter(grad_w_out_part.astype(jnp.bfloat16), 'dp', scatter_dime...  59 us
    reduce_scatter x1, waiting for transfers between devices, per_device(): lax.psum_scatter(grad_w_key_part.astype(jnp.bfloat16), 'dp', scatter_dime...  58.8 us
    reduce_scatter x1, waiting for transfers between devices, per_device(): lax.psum_scatter(grad_w_value_part.astype(jnp.bfloat16), 'dp', scatter_di...  58.6 us
    reduce_scatter x1, waiting for transfers between devices, per_device(): lax.psum_scatter(grad_w_query_part.astype(jnp.bfloat16), 'dp', scatter_di...  58.4 us
    all_gather x1, waiting for transfers between devices, per_device(): lax.all_gather(w_down, 'dp', axis=0, tiled=True)  53.8 us
    reduce_scatter x1, waiting for transfers between devices, per_device(): lax.psum_scatter(contract_cols(mixed_rows, full_out), 'tensor', scatter_d...  52.6 us
    all_gather x1, waiting for transfers between devices, per_device(): lax.all_gather(w_up, 'dp', axis=0, tiled=True)  48.1 us
    psum x1, blocking collectives, per_device(): lax.psum((jnp.sum(grad_normed * scaled_one, axis=0), jnp.sum(grad_normed,...  42.3 us
  transfers between devices with their start and end apart: 20, of which 19 were waited for; matrix products, arithmetic and copies ran while one was open for 22% of the time, Pallas kernels for 0%

commit v1 on v0

v1 whole, which is shorter than its diff:
```python
import functools

import jax
import jax.numpy as jnp
from jax import lax
from jax.experimental import pallas as pl
from jax.experimental.pallas import tpu as pltpu
from jax.sharding import Mesh
from jax.sharding import PartitionSpec as P

HEAD_DIM = 64
LANES = 128
MASKED = -1e30
VMEM_BYTES = 60 * 1024 * 1024
F32 = jnp.float32
BF16 = jnp.bfloat16
DATA = ("a", "h")
TP = ("l", "c")
SWAP = ("c", "h", "l")


def normalize(values):
    center = values - jnp.mean(values, axis=-1, keepdims=True)
    spread = jnp.mean(center * center, axis=-1, keepdims=True)
    inverse = lax.rsqrt(spread + 1e-05)
    return center * inverse, inverse


def norm_back(grad_in, scaled, inverse, gain_vec):
    local_grad = grad_in * gain_vec
    return inverse * (
        local_grad
        - jnp.mean(local_grad, axis=-1, keepdims=True)
        - scaled * jnp.mean(local_grad * scaled, axis=-1, keepdims=True)
    )


def dot_nn(left, right):
    return lax.dot_general(left, right, (((1,), (0,)), ((), ())), preferred_element_type=F32)


def dot_nt(left, right):
    return lax.dot_general(left, right, (((1,), (1,)), ((), ())), preferred_element_type=F32)


def dot_tn(left, right):
    return lax.dot_general(left, right, (((0,), (0,)), ((), ())), preferred_element_type=F32)


def fill_bias(bias, seg_col, seg_row):
    length = bias.shape[0]
    block = min(256, length)
    for first in range(0, length, block):
        keys = lax.broadcasted_iota(jnp.int32, (block, length), 0) + first
        places = lax.broadcasted_iota(jnp.int32, (block, length), 1)
        same = seg_col[first : first + block, :] == seg_row[...]
        bias[first : first + block, :] = jnp.where(same & (keys <= places), 0.0, MASKED)


def head_lanes(values, head):
    lane = lax.broadcasted_iota(jnp.int32, values.shape, 1)
    inside = (lane >= head * HEAD_DIM) & (lane < (head + 1) * HEAD_DIM)
    return jnp.where(inside, values, jnp.zeros_like(values))


def attn_forward_kernel(seg_col, seg_row, q_ref, k_ref, v_ref, mixed_ref, lse_ref, bias, v_t, block):
    length = q_ref.shape[0]
    heads = LANES // HEAD_DIM

    @pl.when(pl.program_id(0) == 0)
    def _():
        fill_bias(bias, seg_col, seg_row)

    v_t[...] = v_ref[...].T
    for place in range(length // block):
        rows = slice(place * block, (place + 1) * block)
        outs = []
        for head in range(heads):
            query = head_lanes(q_ref[rows, :], head)
            scores = []
            peak = None
            for other in range(place + 1):
                keys = slice(other * block, (other + 1) * block)
                part = dot_nt(k_ref[keys, :], query) + bias[keys, rows]
                top = jnp.max(part, axis=0, keepdims=True)
                peak = top if peak is None else jnp.maximum(peak, top)
                scores.append(part)
            total = None
            acc = None
            for other in range(place + 1):
                keys = slice(other * block, (other + 1) * block)
                weight = jnp.exp(scores[other] - peak)
                part_sum = jnp.sum(weight, axis=0, keepdims=True)
                total = part_sum if total is None else total + part_sum
                part_out = dot_nn(
                    v_t[head * HEAD_DIM : (head + 1) * HEAD_DIM, keys], weight.astype(BF16)
                )
                acc = part_out if acc is None else acc + part_out
            outs.append(acc / total)
            lse_ref[0, head : head + 1, rows] = peak + jnp.log(total)
        mixed_ref[rows, :] = jnp.concatenate(outs, axis=0).T.astype(BF16)


def attn_backward_kernel(
    seg_col, seg_row, q_ref, k_ref, v_ref, mixed_ref, lse_ref, g_ref, grads_ref, bias, k_t, delta, dq_t, block
):
    length = q_ref.shape[0]
    heads = LANES // HEAD_DIM
    count = length // block

    @pl.when(pl.program_id(0) == 0)
    def _():
        fill_bias(bias, seg_col, seg_row)

    k_t[...] = k_ref[...].T
    product = (g_ref[...].astype(F32) * mixed_ref[...].astype(F32)).T
    for head in range(heads):
        delta[head : head + 1, :] = jnp.sum(
            product[head * HEAD_DIM : (head + 1) * HEAD_DIM, :], axis=0, keepdims=True
        )
    for other in range(count):
        keys = slice(other * block, (other + 1) * block)
        key_sum = None
        value_sum = None
        for head in range(heads):
            lanes = slice(head * HEAD_DIM, (head + 1) * HEAD_DIM)
            for place in range(other, count):
                rows = slice(place * block, (place + 1) * block)
                query = head_lanes(q_ref[rows, :], head)
                grad = head_lanes(g_ref[rows, :], head)
                scores = dot_nt(k_ref[keys, :], query) + bias[keys, rows]
                probs = jnp.exp(scores - lse_ref[0, head : head + 1, rows])
                grad_probs = dot_nt(v_ref[keys, :], grad)
                grad_scores = (probs * (grad_probs - delta[head : head + 1, rows])).astype(BF16)
                value_part = dot_nn(probs.astype(BF16), grad)
                key_part = dot_nn(grad_scores, query)
                query_part = dot_nn(k_t[lanes, keys], grad_scores)
                value_sum = value_part if value_sum is None else value_sum + value_part
                key_sum = key_part if key_sum is None else key_sum + key_part
                if other == 0:
                    dq_t[lanes, rows] = query_part
                else:
                    dq_t[lanes, rows] += query_part
        grads_ref[1, keys, :] = key_sum.astype(BF16)
        grads_ref[2, keys, :] = value_sum.astype(BF16)
    grads_ref[0] = (dq_t[...].T * HEAD_DIM ** (-0.5)).astype(BF16)


def attn_forward(segments, qkv, width):
    length = qkv.shape[0]
    pairs = width // LANES
    block = min(256, length)
    column = lambda first: pl.BlockSpec((length, LANES), lambda p: (0, first * pairs + p))
    whole = lambda shape: pl.BlockSpec(shape, lambda p: (0, 0))
    return pl.pallas_call(
        functools.partial(attn_forward_kernel, block=block),
        grid=(pairs,),
        in_specs=[whole((length, 1)), whole((1, length)), column(0), column(1), column(2)],
        out_specs=[
            pl.BlockSpec((length, LANES), lambda p: (0, p)),
            pl.BlockSpec((1, 8, length), lambda p: (p, 0, 0)),
        ],
        out_shape=[
            jax.ShapeDtypeStruct((length, width), BF16),
            jax.ShapeDtypeStruct((pairs, 8, length), F32),
        ],
        scratch_shapes=[pltpu.VMEM((length, length), F32), pltpu.VMEM((LANES, length), BF16)],
        compiler_params=pltpu.CompilerParams(vmem_limit_bytes=VMEM_BYTES),
        cost_estimate=pl.CostEstimate(
            flops=4 * length * length * width,
            bytes_accessed=8 * length * width,
            transcendentals=length * length * width // (2 * HEAD_DIM),
        ),
        name="attn_forward",
    )(segments.reshape(length, 1), segments.reshape(1, length), qkv, qkv, qkv)


def attn_backward(segments, qkv, mixed, lse, grad_mixed, width):
    length = qkv.shape[0]
    pairs = width // LANES
    block = min(256, length)
    column = lambda first: pl.BlockSpec((length, LANES), lambda p: (0, first * pairs + p))
    whole = lambda shape: pl.BlockSpec(shape, lambda p: (0, 0))
    return pl.pallas_call(
        functools.partial(attn_backward_kernel, block=block),
        grid=(pairs,),
        in_specs=[
            whole((length, 1)),
            whole((1, length)),
            column(0),
            column(1),
            column(2),
            pl.BlockSpec((length, LANES), lambda p: (0, p)),
            pl.BlockSpec((1, 8, length), lambda p: (p, 0, 0)),
            pl.BlockSpec((length, LANES), lambda p: (0, p)),
        ],
        out_specs=pl.BlockSpec((3, length, LANES), lambda p: (0, 0, p)),
        out_shape=jax.ShapeDtypeStruct((3, length, width), BF16),
        scratch_shapes=[
            pltpu.VMEM((length, length), F32),
            pltpu.VMEM((LANES, length), BF16),
            pltpu.VMEM((8, length), F32),
            pltpu.VMEM((LANES, length), F32),
        ],
        compiler_params=pltpu.CompilerParams(vmem_limit_bytes=VMEM_BYTES),
        cost_estimate=pl.CostEstimate(
            flops=10 * length * length * width,
            bytes_accessed=16 * length * width,
            transcendentals=length * length * width // (2 * HEAD_DIM),
        ),
        name="attn_backward",
    )(segments.reshape(length, 1), segments.reshape(1, length), qkv, qkv, qkv, mixed, lse, grad_mixed)


def mlp_kernel(
    n_ref, g_ref, nt_ref, gt_ref, up_ref, down_ref, b_ref,
    out_ref, gn_ref, gup_ref, gdown_ref, gb_ref,
    out_acc, gn_acc, act, gpre, block
):
    step = pl.program_id(0)
    length = n_ref.shape[0]

    @pl.when(step == 0)
    def _():
        out_acc[...] = jnp.zeros_like(out_acc)
        gn_acc[...] = jnp.zeros_like(gn_acc)

    bias_sum = jnp.zeros(gb_ref.shape, F32)
    for first in range(0, length, block):
        rows = slice(first, first + block)
        unit = dot_nn(n_ref[rows, :], up_ref[...]) + b_ref[...]
        grad = dot_nn(g_ref[rows, :], down_ref[...])
        square = unit * unit
        curve = jnp.tanh(0.7978845608028654 * (unit + 0.044715 * (square * unit)))
        half = 0.5 + 0.5 * curve
        slope = half + (0.5 * unit) * (1.0 - curve * curve) * (
            0.7978845608028654 + (3 * 0.044715 * 0.7978845608028654) * square
        )
        active = (unit * half).astype(BF16)
        grad_pre = (grad * slope).astype(BF16)
        act[rows, :] = active
        gpre[rows, :] = grad_pre
        bias_sum = bias_sum + jnp.sum(grad_pre.astype(F32), axis=0, keepdims=True)
        out_acc[rows, :] += dot_nt(active, down_ref[...])
        gn_acc[rows, :] += dot_nt(grad_pre, up_ref[...])
    gb_ref[...] = bias_sum
    gdown_ref[...] = dot_nn(gt_ref[...], act[...]).astype(BF16)
    gup_ref[...] = dot_nn(nt_ref[...], gpre[...]).astype(BF16)

    @pl.when(step == pl.num_programs(0) - 1)
    def _():
        out_ref[...] = out_acc[...].astype(BF16)
        gn_ref[...] = gn_acc[...].astype(BF16)


def mlp(normed, grad, normed_t, grad_t, weights, bias):
    length, width = normed.shape
    units = weights.shape[1] // 2
    tile = min(256, units)
    tiles = units // tile
    whole = lambda shape: pl.BlockSpec(shape, lambda u: (0, 0), pipeline_mode=pl.Buffered(1))
    return pl.pallas_call(
        functools.partial(mlp_kernel, block=min(256, length)),
        grid=(tiles,),
        in_specs=[
            whole((length, width)),
            whole((length, width)),
            whole((width, length)),
            whole((width, length)),
            pl.BlockSpec((width, tile), lambda u: (0, u)),
            pl.BlockSpec((width, tile), lambda u: (0, tiles + u)),
            pl.BlockSpec((1, tile), lambda u: (0, u)),
        ],
        out_specs=[
            pl.BlockSpec((length, width), lambda u: (0, 0)),
            pl.BlockSpec((length, width), lambda u: (0, 0)),
            pl.BlockSpec((width, tile), lambda u: (0, u)),
            pl.BlockSpec((width, tile), lambda u: (0, u)),
            pl.BlockSpec((1, tile), lambda u: (0, u)),
        ],
        out_shape=[
            jax.ShapeDtypeStruct((length, width), BF16),
            jax.ShapeDtypeStruct((length, width), BF16),
            jax.ShapeDtypeStruct((width, units), BF16),
            jax.ShapeDtypeStruct((width, units), BF16),
            jax.ShapeDtypeStruct((1, units), F32),
        ],
        scratch_shapes=[
            pltpu.VMEM((length, width), F32),
            pltpu.VMEM((length, width), F32),
            pltpu.VMEM((length, tile), BF16),
            pltpu.VMEM((length, tile), BF16),
        ],
        compiler_params=pltpu.CompilerParams(vmem_limit_bytes=VMEM_BYTES),
        cost_estimate=pl.CostEstimate(
            flops=12 * length * width * units,
            bytes_accessed=12 * length * width + 8 * width * units,
            transcendentals=length * units,
        ),
        name="mlp_both",
    )(normed, grad, normed_t, grad_t, weights, weights, bias.reshape(1, units))


def per_device(sizes, *arguments):
    (
        block_input, segment_ids, ln1_gain, ln1_bias, w_query, w_key, w_value, b_query, b_value,
        w_out, b_out, ln2_gain, ln2_bias, w_up, b_up, w_down, b_down, out_grad,
    ) = arguments
    ranks = sizes["h"] * sizes["l"]
    rank = lax.axis_index(TP)
    length = segment_ids.shape[0]
    own_rows = block_input.shape[0]
    head_width = w_query.shape[1]
    unit_width = w_up.shape[1]
    half_units = unit_width // 2
    forth = []
    for group in range(2):
        for part in range(ranks):
            forth.append((group * ranks + part, (part % 2) * ranks + group * (ranks // 2) + part // 2))
    back = [(to, frm) for frm, to in forth]

    def move_in(values):
        return lax.ppermute(values, SWAP, forth)

    def move_out(values):
        return lax.ppermute(values, SWAP, back)

    def partner(values):
        return lax.ppermute(values, "c", [(0, 1), (1, 0)])

    def tp_gather(values):
        if ranks != 2:
            return lax.all_gather(values, TP, axis=0, tiled=True)
        theirs = partner(values)
        return jnp.where(
            rank == 0,
            jnp.concatenate([values, theirs], axis=0),
            jnp.concatenate([theirs, values], axis=0),
        )

    def tp_sum(values):
        if ranks != 2:
            return lax.psum(values.astype(F32), TP)
        return values.astype(F32) + partner(values).astype(F32)

    def own(values):
        return lax.dynamic_slice_in_dim(values, rank * own_rows, own_rows)

    def tp_scatter(values):
        if ranks != 2:
            return lax.psum_scatter(values, TP, scatter_dimension=0, tiled=True).astype(F32)
        theirs = lax.dynamic_slice_in_dim(values, (1 - rank) * own_rows, own_rows)
        return own(values).astype(F32) + partner(theirs).astype(F32)

    def gather_weights(values):
        return lax.all_gather(move_in(values), DATA, axis=0, tiled=True)

    full_attn = gather_weights(jnp.concatenate([w_query, w_key, w_value, w_out], axis=1))
    full_mlp = [
        gather_weights(
            jnp.concatenate(
                [w_up[:, first : first + half_units], w_down[:, first : first + half_units]], axis=1
            )
        )
        for first in (0, half_units)
    ]
    full_qkv = full_attn[:, : 3 * head_width]
    full_out = full_attn[:, 3 * head_width :]
    own_input = move_in(block_input)
    segments = move_in(segment_ids)
    own_grad = move_in(out_grad)
    bias_query = lax.dynamic_slice_in_dim(b_query, rank * head_width, head_width)
    bias_value = lax.dynamic_slice_in_dim(b_value, rank * head_width, head_width)
    bias_up = lax.dynamic_slice_in_dim(b_up, rank * unit_width, unit_width)

    rows_in = tp_gather(own_input).astype(F32)
    grad_rows = tp_gather(own_grad)
    scaled_one, _ = normalize(rows_in)
    normed = (scaled_one * ln1_gain + ln1_bias).astype(BF16)
    scale = HEAD_DIM ** (-0.5)
    factors = jnp.concatenate([jnp.full((head_width,), scale, F32), jnp.ones((2 * head_width,), F32)])
    biases = jnp.concatenate([bias_query * scale, jnp.zeros((head_width,), F32), bias_value])
    qkv = (dot_nn(normed, full_qkv) * factors + biases).astype(BF16)
    mixed, lse = attn_forward(segments, qkv, head_width)
    attended = tp_sum(dot_nt(mixed, full_out).astype(BF16))
    hidden = rows_in + attended + b_out
    scaled_two, inverse_two = normalize(hidden)
    normed_two = (scaled_two * ln2_gain + ln2_bias).astype(BF16)
    normed_two_t = normed_two.T
    grad_rows_t = grad_rows.T

    out_parts, gn_parts, up_parts, down_parts, bias_parts = [], [], [], [], []
    for index, first in enumerate((0, half_units)):
        results = mlp(
            normed_two, grad_rows, normed_two_t, grad_rows_t, full_mlp[index],
            bias_up[first : first + half_units],
        )
        for values, store in zip(results, (out_parts, gn_parts, up_parts, down_parts, bias_parts)):
            store.append(values)
    gn_part = (gn_parts[0].astype(F32) + gn_parts[1].astype(F32)).astype(BF16)
    out_part = (out_parts[0].astype(F32) + out_parts[1].astype(F32)).astype(BF16)
    output = move_out((own(hidden) + tp_scatter(out_part) + b_down).astype(BF16))

    grad_normed_two = tp_sum(gn_part)
    grad_hidden = grad_rows.astype(F32) + norm_back(grad_normed_two, scaled_two, inverse_two, ln2_gain)
    grad_attended = grad_hidden.astype(BF16)
    grad_mixed = dot_nn(grad_attended, full_out).astype(BF16)
    grad_out_part = dot_tn(grad_attended, mixed).astype(BF16)

    def scatter_weights(values):
        return move_out(lax.psum_scatter(values, DATA, scatter_dimension=0, tiled=True)).astype(F32)

    early = scatter_weights(jnp.concatenate(up_parts + down_parts + [grad_out_part], axis=1))
    grad_w_up = early[:, :unit_width]
    grad_w_down = early[:, unit_width : 2 * unit_width]
    grad_w_out = early[:, 2 * unit_width :]

    grads = attn_backward(segments, qkv, mixed, lse, grad_mixed, head_width)
    late = scatter_weights(
        jnp.concatenate([dot_tn(normed, grads[place]).astype(BF16) for place in range(3)], axis=1)
    )
    grad_normed_part = (
        dot_nt(grads[0], full_qkv[:, :head_width])
        + dot_nt(grads[1], full_qkv[:, head_width : 2 * head_width])
        + dot_nt(grads[2], full_qkv[:, 2 * head_width :])
    ).astype(BF16)
    grad_normed = tp_scatter(grad_normed_part)
    own_scaled, own_inverse = normalize(own_input.astype(F32))
    grad_own = own(grad_hidden) + norm_back(grad_normed, own_scaled, own_inverse, ln1_gain)
    grad_input = move_out(grad_own.astype(BF16))

    def place_part(values, full):
        return lax.dynamic_update_slice_in_dim(
            jnp.zeros((full,), F32), values, rank * values.shape[0], 0
        )

    width = ln1_gain.shape[0]
    share = 1.0 / ranks
    sums = jnp.concatenate(
        [
            jnp.sum(grad_normed * own_scaled, axis=0),
            jnp.sum(grad_normed, axis=0),
            place_part(jnp.sum(grads[0].astype(F32), axis=0), width),
            place_part(jnp.sum(grads[2].astype(F32), axis=0), width),
            jnp.sum(grad_hidden, axis=0) * share,
            jnp.sum(grad_normed_two * scaled_two, axis=0) * share,
            jnp.sum(grad_normed_two, axis=0) * share,
            jnp.sum(own_grad.astype(F32), axis=0),
            place_part(jnp.concatenate(bias_parts, axis=1)[0], b_up.shape[0]),
        ]
    )
    sums = lax.psum(sums, ("a", "c", "h", "l"))
    small = [sums[place * width : (place + 1) * width] for place in range(8)]
    return (
        output, grad_input, small[0], small[1],
        late[:, :head_width], late[:, head_width : 2 * head_width], late[:, 2 * head_width :],
        small[2], small[3], grad_w_out, small[4], small[5], small[6], grad_w_up,
        sums[8 * width :], grad_w_down, small[7],
    )


def solution(mesh):
    groups, ranks = mesh.shape["dp"], mesh.shape["tensor"]
    sizes = {"a": groups // 2, "c": 2, "h": 2, "l": ranks // 2}
    fine = Mesh(mesh.devices.reshape(tuple(sizes.values())), tuple(sizes))
    rows = P(("a", "c", "h", "l"), None)
    block = P(("a", "c"), ("h", "l"))
    return jax.shard_map(
        functools.partial(per_device, sizes),
        mesh=fine,
        in_specs=(
            rows, P(("a", "c")), P(), P(), block, block, block, P(), P(), block, P(), P(), P(),
            block, P(), block, P(), rows,
        ),
        out_specs=(
            rows, rows, P(), P(), block, block, block, P(), P(), block, P(), P(), P(), block, P(),
            block, P(),
        ),
        check_vma=False,
    )
```

time: 1050 us -> 640 us (0.61)
  waiting for transfers between devices: 703 us -> 331 us
  matrix products: 183 us -> 28.2 us
  Pallas kernels: 0 us -> 89.6 us
  local copies, waits for them, and re-layouts: 28.8 us -> 56.7 us
  other arithmetic: 63.3 us -> 40.1 us
  starting transfers between devices: 1.95 us -> 24.8 us
    reduce_scatter x9 -> x1, waiting for transfers between devices: 394 us -> 96.2 us  [scatter_weights(): lax.psum_scatter(values, DATA, scatter_dimension=0, tiled=True)]
    all_gather x10 -> x3, waiting for transfers between devices: 304 us -> 108 us  [gather_weights(): return lax.all_gather(move_in(values), DATA, axis=0, tiled=True)]
    dot_general x32 -> x10, matrix products: 183 us -> 28.2 us  [the longest x2 12.5 us: dot_nn(): lax.dot_general(left, right, (((1,), (0,)), ((), ())), preferred_element_...]
    pallas_call x0 -> x4, Pallas kernels: none -> 89.6 us  [the longest x2 48.9 us: mlp(): pl.pallas_call(functools.partial(mlp_kernel, block=min(256, length)), gri...]
    unnamed x21 -> x6, waiting for transfers between devices: 4.54 us -> 89.9 us
    ppermute x0 -> x16, waiting for transfers between devices: none -> 37.3 us  [the longest x6 27.9 us: move_in(): return lax.ppermute(values, SWAP, forth)]
    ppermute x0 -> x16, starting transfers between devices: none -> 24.6 us  [the longest x6 13.4 us: move_in(): return lax.ppermute(values, SWAP, forth)]
    convert_element_type x12 -> x5, other arithmetic: 34.2 us -> 11.6 us  [the longest x1 3.09 us: per_device(): grad_input = move_out(grad_own.astype(BF16))]
  transfers between devices with their start and end apart: 20 -> 21, of which waited for: 19 -> 12; matrix products, arithmetic and copies ran while one was open for 22% -> 16% of each run, Pallas kernels for 0% -> 10%
where the time goes in v1:
time: 640 us; the launch traced here: 629 us
  waiting for transfers between devices  331 us (52%)
  Pallas kernels  89.6 us (14%)
  local copies, waits for them, and re-layouts  56.7 us (9%)
  blocking collectives  43.7 us (7%)
  other arithmetic  40.1 us (6%)
  matrix products  28.2 us (4%)
  starting transfers between devices  24.8 us (4%)
  between operations  15 us (2%)
    all_gather x3, waiting for transfers between devices, gather_weights(): return lax.all_gather(move_in(values), DATA, axis=0, tiled=True)  108 us
    reduce_scatter x1, waiting for transfers between devices, scatter_weights(): lax.psum_scatter(values, DATA, scatter_dimension=0, tiled=True)  96.2 us
    unnamed x6, waiting for transfers between devices  89.9 us
    pallas_call x2, Pallas kernels, mlp(): pl.pallas_call(functools.partial(mlp_kernel, block=min(256, length)), gri...  48.9 us
    psum x1, blocking collectives, per_device(): sums = lax.psum(sums, ('a', 'c', 'h', 'l'))  43.7 us
    ppermute x6, waiting for transfers between devices, move_in(): return lax.ppermute(values, SWAP, forth)  27.9 us
    unnamed x94, local copies, waits for them, and re-layouts  27.7 us
    pallas_call x1, Pallas kernels, attn_backward(): pl.pallas_call(functools.partial(attn_backward_kernel, block=block), grid...  24.3 us
  transfers between devices with their start and end apart: 21, of which 12 were waited for; matrix products, arithmetic and copies ran while one was open for 16% of the time, Pallas kernels for 10%

profile of v1, /device:TPU:10, one launch (start us, length us, event | category | flops | bytes accessed | tf_op | source)
XLA Modules:
  0.0 628.9 jit_solution(5657479776740298102)
XLA Ops:
  8.4 1.9 collective-permute-start.3
  10.3 5.8 collective-permute-done.3
  18.9 1.9 collective-permute-start.8
  20.8 5.8 collective-permute-done.8
  27.9 1.9 collective-permute-start
  29.8 14.2 %collective-permute-done = bf16[512,1024]{0,1:T(8,128)(2,1)S(1)} collective-permute-done((bf16[512,1024]{0,1:T(8,128)(2,1)S(1)}, bf16[512,1024]{0,1:T(8,128)(2,1)S(1)}, u32[]{:S(2)}, u32[]{:S(2)}) %collective-permute-start) | collective-permute-done | bytes 1048608 | tf_op jit(solution)/shard_map/ppermute | solution.py:323
  44.8 2.0 collective-permute-start.7
  46.8 3.6 collective-permute-start.2
  53.9 2.2 collective-permute-done.2
  59.5 2.3 fusion.5
  61.9 34.0 %all-gather.4.cloned.1.call-done = bf16[1024,2048]{1,0:T(8,128)(2,1)} async-done(((bf16[64,2048]{1,0:T(8,128)(2,1)}), bf16[1024,2048]{1,0:T(8,128)(2,1)}) %all-gather.4.cloned.1.call-update) | async-done | bytes 4194320 | tf_op jit(solution)/shard_map/all_gather | solution.py:356
  95.8 7.8 %add_convert_fusion.q_ref.k_ref.v_ref = bf16[1024,1536]{1,0:T(8,128)(2,1)} fusion(bf16[1024,1024]{0,1:T(8,128)(2,1)} %fusion.5, bf16[1024,2048]{1,0:T(8,128)(2,1)} %all-gather.4.cloned.1.call-done, f32[1536]{0:T(1024)S(1)} %pad_maximum_fusion.4, f32[1536]{0:T(1024)S(1)} %copy-done.37), kind=kOutput, calls=%fused_computation | convolution fusion | flops 3225944064 | bytes 8400896 | tf_op jit(solution)/shard_map/dot_general | solution.py:39
  103.6 16.4 %attn_forward.1 = (bf16[1024,512]{1,0:T(8,128)(2,1)}, f32[4,8,1024]{2,1,0:T(8,128)}) custom-call(s32[1024,1]{1,0:T(8,128)} %copy.76.seg_col, s32[1,1024]{1,0:T(1,128)} %bitcast.35, bf16[1024,1536]{1,0:T(8,128)(2,1)} %add_convert_fusion.q_ref.k_ref.v_ref, bf16[1024,1536]{1,0:T(8,128)(2,1)} %add_convert_fusion.q_ref.k_ref.v_ref, ...), custom_call_target="tpu_custom_call" | custom-call | flops 2147483648 | bytes 4194304 | tf_op jit(solution)/shard_map/attn_forward/pallas_call | solution.py:155
  120.0 4.1 convolution_convert_fusion
  125.2 4.3 collective-permute-done.6
  129.5 3.2 maximum_select_fusion.1
  132.8 2.6 copy.79.g_ref
  135.4 4.8 fusion.40
  142.9 2.7 copy.78.n_ref
  145.5 4.1 fusion.54.nt_ref
  149.7 23.5 %all-gather.8.cloned.1.call-done.up_ref.down_ref = bf16[1024,2048]{1,0:T(8,128)(2,1)} async-done(((bf16[64,2048]{1,0:T(8,128)(2,1)}), bf16[1024,2048]{1,0:T(8,128)(2,1)}) %all-gather.8.cloned.1.call-update) | async-done | bytes 4194320 | tf_op jit(solution)/shard_map/all_gather | solution.py:356
  173.2 24.4 %mlp_both.3 = (bf16[1024,1024]{1,0:T(8,128)(2,1)}, bf16[1024,1024]{1,0:T(8,128)(2,1)}, bf16[1024,1024]{1,0:T(8,128)(2,1)}, bf16[1024,1024]{1,0:T(8,128)(2,1)}, f32[1,1024]{1,0:T(1,128)}) custom-call(bf16[1024,1024]{1,0:T(8,128)(2,1)} %copy.78.n_ref, bf16[1024,1024]{1,0:T(8,128)(2,1)} %copy.79.g_ref, bf16[1024,1024]{1,0:T(8,128)(2,1)} %fusion.54.nt_ref, ...), custom_call_target="tpu_custom_call" | custom-call | flops 12884901888 | bytes 20971520 | tf_op jit(solution)/shard_map/mlp_both/pallas_call | solution.py:262
  197.6 2.9 copy.85
  200.5 50.0 %all-gather.6.cloned.1.call-done.up_ref.down_ref = bf16[1024,2048]{1,0:T(8,128)(2,1)} async-done(((bf16[64,2048]{1,0:T(8,128)(2,1)}), bf16[1024,2048]{1,0:T(8,128)(2,1)}) %all-gather.6.cloned.1.call-update) | async-done | bytes 4194320 | tf_op jit(solution)/shard_map/all_gather | solution.py:356
  250.5 24.5 %mlp_both.2 = (bf16[1024,1024]{1,0:T(8,128)(2,1)}, bf16[1024,1024]{1,0:T(8,128)(2,1)}, bf16[1024,1024]{1,0:T(8,128)(2,1)}, bf16[1024,1024]{1,0:T(8,128)(2,1)}, f32[1,1024]{1,0:T(1,128)}) custom-call(bf16[1024,1024]{1,0:T(8,128)(2,1)} %copy.78.n_ref, bf16[1024,1024]{1,0:T(8,128)(2,1)} %copy.79.g_ref, bf16[1024,1024]{1,0:T(8,128)(2,1)} %fusion.54.nt_ref, ...), custom_call_target="tpu_custom_call" | custom-call | flops 12884901888 | bytes 20971520 | tf_op jit(solution)/shard_map/mlp_both/pallas_call | solution.py:262
  275.0 4.0 copy.84
  279.0 2.7 add_convert_fusion.2
  290.1 2.4 multiply_reduce_fusion
  292.5 2.5 fusion.39
  295.0 1.9 copy-done.7
  297.0 2.3 fusion.26
  299.4 4.7 convolution_convert_fusion.5.g_ref
  304.1 24.3 %attn_backward.1 = bf16[3,1024,512]{2,1,0:T(8,128)(2,1)} custom-call(s32[1024,1]{1,0:T(8,128)} %copy.76.seg_col, s32[1,1024]{1,0:T(1,128)} %bitcast.36, bf16[1024,1536]{1,0:T(8,128)(2,1)} %add_convert_fusion.q_ref.k_ref.v_ref, bf16[1024,1536]{1,0:T(8,128)(2,1)} %add_convert_fusion.q_ref.k_ref.v_ref, bf16[1024,1536]{1,0:T(8,128)(2,1)} %add_convert_fusion.q_ref.k_ref.v_ref, ...), custom_call_target="tpu_custom_call" | custom-call | flops 5368709120 | bytes 8388608 | tf_op jit(solution)/shard_map/attn_backward/pallas_call | solution.py:184
  328.5 2.7 convolution_convert_fusion.2
  333.8 1.9 pad_maximum_fusion
  335.7 4.7 copy.100
  342.1 2.9 copy.80
  345.0 4.2 copy.83
  349.3 2.8 add_convert_fusion.3
  362.1 4.5 fusion.21
  366.6 3.1 fusion.20
  369.7 2.1 collective-permute-start.13
  371.8 3.4 collective-permute-start.10
  375.3 96.2 %reduce-scatter.5.cloned.1.call-done = bf16[64,4608]{1,0:T(8,128)(2,1)} async-done(((bf16[1024,4608]{1,0:T(8,128)(2,1)}), bf16[64,4608]{1,0:T(8,128)(2,1)}) %reduce-scatter.5.cloned.1.call-update) | async-done | bytes 589840 | tf_op jit(solution)/shard_map/reduce_scatter | solution.py:411
  473.4 43.7 %psum.7 = f32[12288]{0:T(1024)S(1)} all-reduce(f32[12288]{0:T(1024)S(1)} %constant_dynamic-update-slice_fusion.8), channel_id=1, replica_groups=mesh['a'=8,'c'=2,'h'=2,'l'=1] {'a','c','h','l'}, use_global_device_ids=true, to_apply=%region_18.19 | all-reduce | flops 12288 | bytes 98304 | tf_op jit(solution)/shard_map/psum | solution.py:452
  517.7 89.9 %reduce-scatter.7.cloned.1.call-done = bf16[64,1536]{1,0:T(8,128)(2,1)} async-done(((bf16[1024,1536]{1,0:T(8,128)(2,1)}), bf16[64,1536]{1,0:T(8,128)(2,1)}) %reduce-scatter.7.cloned.1.call-update) | async-done | bytes 196624
  608.7 1.9 collective-permute-start.14
  613.9 3.9 collective-permute-done.14
  (172 shorter events, 50.1 us)
Async XLA Ops:
  7.2 20.2 %copy-start.18 = (bf16[512,1024]{1,0:T(8,128)(2,1)S(1)}, bf16[512,1024]{1,0:T(8,128)(2,1)}, u32[]{:S(2)}) copy-start(bf16[512,1024]{1,0:T(8,128)(2,1)} %param.18) | copy-start | bytes 3145732
  7.2 39.6 %copy-start.36 = (s32[1024]{0:T(1024)S(1)}, s32[1024]{0:T(1024)}, u32[]{:S(2)}) copy-start(s32[1024]{0:T(1024)} %param.19) | copy-start | bytes 12292
  7.2 43.3 %copy-start.19 = (bf16[512,1024]{1,0:T(8,128)(2,1)S(1)}, bf16[512,1024]{1,0:T(8,128)(2,1)}, u32[]{:S(2)}) copy-start(bf16[512,1024]{1,0:T(8,128)(2,1)} %param.35) | copy-start | bytes 3145732
  7.2 88.6 %all-gather.4.cloned.1.call-start = ((), (), s32[]{:S(2)}) async-start(), calls=%async_computation.2 | async-start | bytes 4456448 | tf_op jit(solution)/shard_map/all_gather | solution.py:356
  8.4 7.7 %collective-permute-start.3 = (bf16[64,2048]{1,0:T(8,128)(2,1)S(1)}, bf16[64,2048]{1,0:T(8,128)(2,1)S(1)}, u32[]{:S(2)}, u32[]{:S(2)}) collective-permute-start(bf16[64,2048]{1,0:T(8,128)(2,1)S(1)} %pad_maximum_fusion.1), channel_id=1, source_target_pairs={{0,0},{1,2},{2,1},{3,3},{4,4},{5,6},{6,5},{7,7},{8,8},{9,10},{10,9... | collective-permute-start | bytes 786440 | tf_op jit(solution)/shard_map/ppermute | solution.py:323
  16.8 156.4 %all-gather.8.cloned.1.call-start = ((), (), s32[]{:S(2)}) async-start(), calls=%async_computation.4 | async-start | bytes 4456448 | tf_op jit(solution)/shard_map/all_gather | solution.py:356
  17.8 35.9 %copy-start.33 = (f32[1024]{0:T(1024)S(1)}, f32[1024]{0:T(1024)}, u32[]{:S(2)}) copy-start(f32[1024]{0:T(1024)} %param.26) | copy-start | bytes 12292
  17.8 36.0 %copy-start.34 = (f32[1024]{0:T(1024)S(1)}, f32[1024]{0:T(1024)}, u32[]{:S(2)}) copy-start(f32[1024]{0:T(1024)} %param.25) | copy-start | bytes 12292
  18.9 7.7 %collective-permute-start.8 = (bf16[64,2048]{1,0:T(8,128)(2,1)S(1)}, bf16[64,2048]{1,0:T(8,128)(2,1)S(1)}, u32[]{:S(2)}, u32[]{:S(2)}) collective-permute-start(bf16[64,2048]{1,0:T(8,128)(2,1)S(1)} %pad_maximum_fusion.3), channel_id=1, source_target_pairs={{0,0},{1,2},{2,1},{3,3},{4,4},{5,6},{6,5},{7,7},{8,8},{9,10},{10,9... | collective-permute-start | bytes 786440 | tf_op jit(solution)/shard_map/ppermute | solution.py:323
  27.3 223.2 %all-gather.6.cloned.1.call-start = ((), (), s32[]{:S(2)}) async-start(), calls=%async_computation.3 | async-start | bytes 4456448 | tf_op jit(solution)/shard_map/all_gather | solution.py:356
  27.9 16.1 %collective-permute-start = (bf16[512,1024]{0,1:T(8,128)(2,1)S(1)}, bf16[512,1024]{0,1:T(8,128)(2,1)S(1)}, u32[]{:S(2)}, u32[]{:S(2)}) collective-permute-start(bf16[512,1024]{0,1:T(8,128)(2,1)S(1)} %copy.75), channel_id=1, source_target_pairs={{0,0},{1,2},{2,1},{3,3},{4,4},{5,6},{6,5},{7,7},{8,8},{9,10},{10,9... | collective-permute-start | bytes 3145736 | tf_op jit(solution)/shard_map/ppermute | solution.py:323
  44.0 13.9 %collective-permute-start.1 = (bf16[512,1024]{0,1:T(8,128)(2,1)S(1)}, bf16[512,1024]{0,1:T(8,128)(2,1)S(1)}, u32[]{:S(2)}, u32[]{:S(2)}) collective-permute-start(bf16[512,1024]{0,1:T(8,128)(2,1)S(1)} %collective-permute-done), channel_id=1, source_target_pairs={{0,2},{2,0},{1,3},{3,1},{4,6},{6,4},{5,7},{7,5},{8,10},{10,8},{9,1... | collective-permute-start | bytes 3145736 | tf_op jit(solution)/shard_map/ppermute | solution.py:329
  44.8 14.8 %copy-start.24 = (f32[1024]{0:T(1024)S(1)}, f32[1024]{0:T(1024)}, u32[]{:S(2)}) copy-start(f32[1024]{0:T(1024)} %param.20) | copy-start | bytes 12292
  44.8 14.8 %copy-start.32 = (f32[1024]{0:T(1024)S(1)}, f32[1024]{0:T(1024)}, u32[]{:S(2)}) copy-start(f32[1024]{0:T(1024)} %param.21) | copy-start | bytes 12292
  44.8 12.4 %collective-permute-start.7 = (bf16[64,2048]{1,0:T(8,128)(2,1)}, bf16[64,2048]{1,0:T(8,128)(2,1)S(1)}, u32[]{:S(2)}, u32[]{:S(2)}) collective-permute-start(bf16[64,2048]{1,0:T(8,128)(2,1)} %pad_maximum_fusion.2), channel_id=1, source_target_pairs={{0,0},{1,2},{2,1},{3,3},{4,4},{5,6},{6,5},{7,7},{8,8},{9,10},{10,9... | collective-permute-start | bytes 786440 | tf_op jit(solution)/shard_map/ppermute | solution.py:323
  46.8 9.3 %collective-permute-start.2 = (s32[1024]{0:T(1024)S(1)}, s32[1024]{0:T(1024)S(1)}, u32[]{:S(2)}, u32[]{:S(2)}) collective-permute-start(s32[1024]{0:T(1024)S(1)} %copy-done.36), channel_id=1, source_target_pairs={{0,0},{1,2},{2,1},{3,3},{4,4},{5,6},{6,5},{7,7},{8,8},{9,10},{10,9... | collective-permute-start | bytes 12296 | tf_op jit(solution)/shard_map/ppermute | solution.py:323
  51.8 72.3 %collective-permute-start.5 = (bf16[512,1024]{0,1:T(8,128)(2,1)}, bf16[512,1024]{0,1:T(8,128)(2,1)S(1)}, u32[]{:S(2)}, u32[]{:S(2)}) collective-permute-start(bf16[512,1024]{0,1:T(8,128)(2,1)} %copy.77), channel_id=1, source_target_pairs={{0,0},{1,2},{2,1},{3,3},{4,4},{5,6},{6,5},{7,7},{8,8},{9,10},{10,9... | collective-permute-start | bytes 3145736 | tf_op jit(solution)/shard_map/ppermute | solution.py:323
  56.1 5.8 copy-start.26
  57.9 413.6 %reduce-scatter.5.cloned.1.call-start = ((), (), s32[]{:S(2)}) async-start(), calls=%async_computation.5 | async-start | bytes 10027008 | tf_op jit(solution)/shard_map/reduce_scatter | solution.py:411
  57.9 3.9 copy-start.4
  58.6 37.2 %copy-start.37 = (f32[1536]{0:T(1024)S(1)}, f32[1536]{0:T(1024)}, u32[]{:S(2)}) copy-start(f32[1536]{0:T(1024)} %constant.41.clone.1) | copy-start | bytes 18436
  120.0 4.7 copy-start.29
  124.1 11.3 %collective-permute-start.4 = (bf16[1024,1024]{0,1:T(8,128)(2,1)}, bf16[1024,1024]{0,1:T(8,128)(2,1)}, u32[]{:S(2)}, u32[]{:S(2)}) collective-permute-start(bf16[1024,1024]{0,1:T(8,128)(2,1)} %convolution_convert_fusion), channel_id=1, source_target_pairs={{0,2},{2,0},{1,3},{3,1},{4,6},{6,4},{5,7},{7,5},{8,10},{10,8},{9,1... | collective-permute-start | bytes 6291464 | tf_op jit(solution)/shard_map/ppermute | solution.py:329
  124.1 5.4 collective-permute-start.6
  132.7 7.5 %copy-start.2 = (bf16[1024,1024]{0,1:T(8,128)(2,1)}, bf16[1024,1024]{0,1:T(8,128)(2,1)S(1)}, u32[]{:S(2)}) copy-start(bf16[1024,1024]{0,1:T(8,128)(2,1)S(1)} %maximum_select_fusion.1) | copy-start | bytes 6291460
  132.8 2.7 copy-start.28
  279.0 2.8 copy-start.17
  281.7 2.3 copy-start.15
  281.7 7.8 %collective-permute-start.11 = (bf16[1024,1024]{0,1:T(8,128)(2,1)S(1)}, bf16[1024,1024]{0,1:T(8,128)(2,1)S(1)}, u32[]{:S(2)}, u32[]{:S(2)}) collective-permute-start(bf16[1024,1024]{0,1:T(8,128)(2,1)S(1)} %add_convert_fusion.2), channel_id=1, source_target_pairs={{0,2},{2,0},{1,3},{3,1},{4,6},{6,4},{5,7},{7,5},{8,10},{10,8},{9,1... | collective-permute-start | bytes 6291464 | tf_op jit(solution)/shard_map/ppermute | solution.py:329
  283.4 2.3 copy-start.16
  285.7 2.3 copy-start.14
  287.2 2.8 copy-start.1
  289.6 2.9 copy-start.3
  292.5 4.5 copy-start.35
  299.3 308.2 %reduce-scatter.7.cloned.1.call-start = ((), (), s32[]{:S(2)}) async-start(), calls=%async_computation.6 | async-start | bytes 3342336
  304.1 24.3 %copy-start.13 = (bf16[1024,1024]{0,1:T(8,128)(2,1)S(1)}, bf16[1024,1024]{0,1:T(8,128)(2,1)}, u32[]{:S(2)}) copy-start(bf16[1024,1024]{0,1:T(8,128)(2,1)} %fusion.5) | copy-start | bytes 6291460
  328.5 2.7 copy-start.5
  349.2 4.8 copy-start.6
  349.2 4.8 copy-start.12
  352.0 3.3 copy-start.9
  353.1 7.8 %collective-permute-start.9 = (bf16[512,1024]{0,1:T(8,128)(2,1)}, bf16[512,1024]{0,1:T(8,128)(2,1)}, u32[]{:S(2)}, u32[]{:S(2)}) collective-permute-start(bf16[512,1024]{0,1:T(8,128)(2,1)} %constant_dynamic-slice_fusion), channel_id=1, source_target_pairs={{0,2},{2,0},{1,3},{3,1},{4,6},{6,4},{5,7},{7,5},{8,10},{10,8},{9,1... | collective-permute-start | bytes 3145736 | tf_op jit(solution)/shard_map/ppermute | solution.py:329
  358.0 4.1 copy-start.27
  359.1 3.0 collective-permute-start.12
  361.0 5.6 copy-start.8
  369.7 241.6 %collective-permute-start.13 = (bf16[512,1024]{0,1:T(8,128)(2,1)}, bf16[512,1024]{0,1:T(8,128)(2,1)S(1)}, u32[]{:S(2)}, u32[]{:S(2)}) collective-permute-start(bf16[512,1024]{0,1:T(8,128)(2,1)} %fusion.20), channel_id=1, source_target_pairs={{0,0},{2,1},{1,2},{3,3},{4,4},{6,5},{5,6},{7,7},{8,8},{10,9},{9,10... | collective-permute-start | bytes 3145736 | tf_op jit(solution)/shard_map/ppermute | solution.py:326
  371.8 240.8 %collective-permute-start.10 = (bf16[512,1024]{0,1:T(8,128)(2,1)}, bf16[512,1024]{0,1:T(8,128)(2,1)S(1)}, u32[]{:S(2)}, u32[]{:S(2)}) collective-permute-start(bf16[512,1024]{0,1:T(8,128)(2,1)} %get-tuple-element.125), channel_id=1, source_target_pairs={{0,0},{2,1},{1,2},{3,3},{4,4},{6,5},{5,6},{7,7},{8,8},{10,9},{9,10... | collective-permute-start | bytes 3145736 | tf_op jit(solution)/shard_map/ppermute | solution.py:326
  471.5 148.7 %collective-permute-start.15 = (bf16[64,4608]{1,0:T(8,128)(2,1)}, bf16[64,4608]{1,0:T(8,128)(2,1)S(1)}, u32[]{:S(2)}, u32[]{:S(2)}) collective-permute-start(bf16[64,4608]{1,0:T(8,128)(2,1)} %reduce-scatter.5.cloned.1.call-done), channel_id=1, source_target_pairs={{0,0},{2,1},{1,2},{3,3},{4,4},{6,5},{5,6},{7,7},{8,8},{10,9},{9,10... | collective-permute-start | bytes 1769480 | tf_op jit(solution)/shard_map/ppermute | solution.py:326
  608.7 9.1 %collective-permute-start.14 = (bf16[64,1536]{0,1:T(8,128)(2,1)S(1)}, bf16[64,1536]{0,1:T(8,128)(2,1)S(1)}, u32[]{:S(2)}, u32[]{:S(2)}) collective-permute-start(bf16[64,1536]{0,1:T(8,128)(2,1)S(1)} %copy.101), channel_id=1, source_target_pairs={{0,0},{2,1},{1,2},{3,3},{4,4},{6,5},{5,6},{7,7},{8,8},{10,9},{9,10... | collective-permute-start | bytes 589832 | tf_op jit(solution)/shard_map/ppermute | solution.py:326
  (11 other events, 16.0 us)
Sparse Core Ops, SparseCore 0:
  16.9 78.8 all-gather.3
  98.6 74.5 all-gather.7
  176.0 74.5 all-gather.5
  299.4 171.9 reduce-scatter.4
  477.1 130.4 reduce-scatter.6

commit v2 on v1

--- a/solution.py
+++ b/solution.py
@@ -14,9 +14,9 @@
 VMEM_BYTES = 60 * 1024 * 1024
 F32 = jnp.float32
 BF16 = jnp.bfloat16
-DATA = ("a", "h")
 TP = ("l", "c")
 SWAP = ("c", "h", "l")
+CUBE = ("a", "c", "h")
 
 
 def normalize(values):
@@ -212,24 +212,135 @@
     )(segments.reshape(length, 1), segments.reshape(1, length), qkv, qkv, qkv, mixed, lse, grad_mixed)
 
 
-def mlp_kernel(
-    n_ref, g_ref, nt_ref, gt_ref, up_ref, down_ref, b_ref,
-    out_ref, gn_ref, gup_ref, gdown_ref, gb_ref,
-    out_acc, gn_acc, act, gpre, block
-):
+def piece_sizes(rows):
+    quarter = rows // 4
+    return (quarter, quarter, quarter, quarter // 2, quarter // 2)
+
+
+def piece_slices(rows):
+    slices, first = [], 0
+    for size in piece_sizes(rows):
+        slices.append(slice(first, first + size))
+        first += size
+    return slices
+
+
+def whole_spec(shape, **options):
+    return pl.BlockSpec(shape, lambda step: (0,) * len(shape), **options)
+
+
+def norm_kernel(*refs, residual):
+    if residual:
+        x_ref, own_ref, other_ref, shift_ref, gain_ref, bias_ref, n_ref, nt_ref, hidden_ref = refs
+        values = (
+            x_ref[...].astype(F32)
+            + (own_ref[...].astype(F32) + other_ref[...].astype(F32))
+            + shift_ref[...]
+        )
+        hidden_ref[...] = values
+    else:
+        x_ref, gain_ref, bias_ref, n_ref, nt_ref = refs
+        values = x_ref[...].astype(F32)
+    scaled, _ = normalize(values)
+    normed = (scaled * gain_ref[...] + bias_ref[...]).astype(BF16)
+    n_ref[...] = normed
+    nt_ref[...] = normed.T
+
+
+def norm_rows(x, gain, bias, partials=None, shift=None):
+    length, width = x.shape
+    block = min(256, length)
+    row = pl.BlockSpec((block, width), lambda step: (step, 0))
+    vector = whole_spec((1, width))
+    residual = partials is not None
+    operands = [x] + (list(partials) + [shift.reshape(1, width)] if residual else [])
+    operands += [gain.reshape(1, width), bias.reshape(1, width)]
+    return pl.pallas_call(
+        functools.partial(norm_kernel, residual=residual),
+        grid=(length // block,),
+        in_specs=[row] + ([row, row, vector] if residual else []) + [vector, vector],
+        out_specs=[row, pl.BlockSpec((width, block), lambda step: (0, step))]
+        + ([row] if residual else []),
+        out_shape=[
+            jax.ShapeDtypeStruct((length, width), BF16),
+            jax.ShapeDtypeStruct((width, length), BF16),
+        ]
+        + ([jax.ShapeDtypeStruct((length, width), F32)] if residual else []),
+        compiler_params=pltpu.CompilerParams(vmem_limit_bytes=VMEM_BYTES),
+        cost_estimate=pl.CostEstimate(
+            flops=20 * length * width, bytes_accessed=14 * length * width, transcendentals=length
+        ),
+        name="norm_two" if residual else "norm_one",
+    )(*operands)
+
+
+def norm_back_kernel(hidden_ref, g_ref, own_ref, other_ref, gain_ref, grad_ref, low_ref, sums_ref):
+    scaled, inverse = normalize(hidden_ref[...])
+    incoming = own_ref[...].astype(F32) + other_ref[...].astype(F32)
+    grad = g_ref[...].astype(F32) + norm_back(incoming, scaled, inverse, gain_ref[...])
+    grad_ref[...] = grad
+    low_ref[...] = grad.astype(BF16)
+
+    @pl.when(pl.program_id(0) == 0)
+    def _():
+        sums_ref[...] = jnp.zeros_like(sums_ref)
+
+    sums_ref[0:1, :] += jnp.sum(grad, axis=0, keepdims=True)
+    sums_ref[1:2, :] += jnp.sum(incoming * scaled, axis=0, keepdims=True)
+    sums_ref[2:3, :] += jnp.sum(incoming, axis=0, keepdims=True)
+
+
+def norm_back_rows(hidden, grad, partials, gain):
+    length, width = hidden.shape
+    block = min(256, length)
+    row = pl.BlockSpec((block, width), lambda step: (step, 0))
+    return pl.pallas_call(
+        norm_back_kernel,
+        grid=(length // block,),
+        in_specs=[row, row, row, row, whole_spec((1, width))],
+        out_specs=[row, row, whole_spec((8, width))],
+        out_shape=[
+            jax.ShapeDtypeStruct((length, width), F32),
+            jax.ShapeDtypeStruct((length, width), BF16),
+            jax.ShapeDtypeStruct((8, width), F32),
+        ],
+        compiler_params=pltpu.CompilerParams(vmem_limit_bytes=VMEM_BYTES),
+        cost_estimate=pl.CostEstimate(
+            flops=30 * length * width, bytes_accessed=16 * length * width, transcendentals=length
+        ),
+        name="norm_two_back",
+    )(hidden, grad, *partials, gain.reshape(1, width))
+
+
+def mlp_kernel(n_ref, g_ref, nt_ref, gt_ref, *refs, block, with_previous):
+    up_refs, down_refs, refs = refs[:5], refs[5:10], refs[10:]
+    if with_previous:
+        (b_ref, before_out, before_gn), refs = refs[:3], refs[3:]
+    else:
+        (b_ref,), refs = refs[:1], refs[1:]
+    (out_ref, gn_ref), grad_refs, refs = refs[:2], refs[2:7], refs[7:]
+    gb_ref, out_acc, gn_acc, act, gpre, up_all, down_all = refs
     step = pl.program_id(0)
-    length = n_ref.shape[0]
+    length, width = n_ref.shape
+    slices = piece_slices(width)
 
     @pl.when(step == 0)
     def _():
-        out_acc[...] = jnp.zeros_like(out_acc)
-        gn_acc[...] = jnp.zeros_like(gn_acc)
-
+        if with_previous:
+            out_acc[...] = before_out[...].astype(F32)
+            gn_acc[...] = before_gn[...].astype(F32)
+        else:
+            out_acc[...] = jnp.zeros_like(out_acc)
+            gn_acc[...] = jnp.zeros_like(gn_acc)
+
+    for piece, up, down in zip(slices, up_refs, down_refs):
+        up_all[piece, :] = up[...]
+        down_all[piece, :] = down[...]
     bias_sum = jnp.zeros(gb_ref.shape, F32)
     for first in range(0, length, block):
         rows = slice(first, first + block)
-        unit = dot_nn(n_ref[rows, :], up_ref[...]) + b_ref[...]
-        grad = dot_nn(g_ref[rows, :], down_ref[...])
+        unit = dot_nn(n_ref[rows, :], up_all[...]) + b_ref[...]
+        grad = dot_nn(g_ref[rows, :], down_all[...])
         square = unit * unit
         curve = jnp.tanh(0.7978845608028654 * (unit + 0.044715 * (square * unit)))
         half = 0.5 + 0.5 * curve
@@ -241,11 +352,14 @@
         act[rows, :] = active
         gpre[rows, :] = grad_pre
         bias_sum = bias_sum + jnp.sum(grad_pre.astype(F32), axis=0, keepdims=True)
-        out_acc[rows, :] += dot_nt(active, down_ref[...])
-        gn_acc[rows, :] += dot_nt(grad_pre, up_ref[...])
+        out_acc[rows, :] += dot_nt(active, down_all[...])
+        gn_acc[rows, :] += dot_nt(grad_pre, up_all[...])
     gb_ref[...] = bias_sum
-    gdown_ref[...] = dot_nn(gt_ref[...], act[...]).astype(BF16)
-    gup_ref[...] = dot_nn(nt_ref[...], gpre[...]).astype(BF16)
+    grad_up = dot_nn(nt_ref[...], gpre[...]).astype(BF16)
+    grad_down = dot_nn(gt_ref[...], act[...]).astype(BF16)
+    for piece, grad_ref in zip(slices, grad_refs):
+        grad_ref[0] = grad_up[piece, :]
+        grad_ref[1] = grad_down[piece, :]
 
     @pl.when(step == pl.num_programs(0) - 1)
     def _():
@@ -253,43 +367,40 @@
         gn_ref[...] = gn_acc[...].astype(BF16)
 
 
-def mlp(normed, grad, normed_t, grad_t, weights, bias):
+def mlp(normed, grad, normed_t, grad_t, pieces, bias, previous):
     length, width = normed.shape
-    units = weights.shape[1] // 2
+    units = pieces[0].shape[1] // 2
     tile = min(256, units)
     tiles = units // tile
-    whole = lambda shape: pl.BlockSpec(shape, lambda u: (0, 0), pipeline_mode=pl.Buffered(1))
-    return pl.pallas_call(
-        functools.partial(mlp_kernel, block=min(256, length)),
+    once = pl.Buffered(1)
+    sizes = piece_sizes(width)
+    at_tile = lambda rows, first: pl.BlockSpec((rows, tile), lambda u: (0, first + u))
+    results = pl.pallas_call(
+        functools.partial(mlp_kernel, block=min(256, length), with_previous=bool(previous)),
         grid=(tiles,),
         in_specs=[
-            whole((length, width)),
-            whole((length, width)),
-            whole((width, length)),
-            whole((width, length)),
-            pl.BlockSpec((width, tile), lambda u: (0, u)),
-            pl.BlockSpec((width, tile), lambda u: (0, tiles + u)),
-            pl.BlockSpec((1, tile), lambda u: (0, u)),
-        ],
-        out_specs=[
-            pl.BlockSpec((length, width), lambda u: (0, 0)),
-            pl.BlockSpec((length, width), lambda u: (0, 0)),
-            pl.BlockSpec((width, tile), lambda u: (0, u)),
-            pl.BlockSpec((width, tile), lambda u: (0, u)),
-            pl.BlockSpec((1, tile), lambda u: (0, u)),
-        ],
-        out_shape=[
-            jax.ShapeDtypeStruct((length, width), BF16),
-            jax.ShapeDtypeStruct((length, width), BF16),
-            jax.ShapeDtypeStruct((width, units), BF16),
-            jax.ShapeDtypeStruct((width, units), BF16),
-            jax.ShapeDtypeStruct((1, units), F32),
-        ],
+            whole_spec((length, width), pipeline_mode=once),
+            whole_spec((length, width), pipeline_mode=once),
+            whole_spec((width, length), pipeline_mode=once),
+            whole_spec((width, length), pipeline_mode=once),
+        ]
+        + [at_tile(size, 0) for size in sizes]
+        + [at_tile(size, tiles) for size in sizes]
+        + [at_tile(1, 0)]
+        + [whole_spec((length, width), pipeline_mode=once) for _ in previous],
+        out_specs=[whole_spec((length, width)), whole_spec((length, width))]
+        + [pl.BlockSpec((2, size, tile), lambda u: (0, 0, u)) for size in sizes]
+        + [at_tile(1, 0)],
+        out_shape=[jax.ShapeDtypeStruct((length, width), BF16)] * 2
+        + [jax.ShapeDtypeStruct((2, size, units), BF16) for size in sizes]
+        + [jax.ShapeDtypeStruct((1, units), F32)],
         scratch_shapes=[
             pltpu.VMEM((length, width), F32),
             pltpu.VMEM((length, width), F32),
             pltpu.VMEM((length, tile), BF16),
             pltpu.VMEM((length, tile), BF16),
+            pltpu.VMEM((width, tile), BF16),
+            pltpu.VMEM((width, tile), BF16),
         ],
         compiler_params=pltpu.CompilerParams(vmem_limit_bytes=VMEM_BYTES),
         cost_estimate=pl.CostEstimate(
@@ -298,7 +409,148 @@
             transcendentals=length * units,
         ),
         name="mlp_both",
-    )(normed, grad, normed_t, grad_t, weights, weights, bias.reshape(1, units))
+    )(normed, grad, normed_t, grad_t, *pieces, *pieces, bias.reshape(1, units), *previous)
+    return results[0], results[1], results[2:7], results[7]
+
+
+def qkv_weight_kernel(nt_ref, grads_ref, *piece_refs):
+    grad = dot_nn(nt_ref[...], grads_ref[0]).astype(BF16)
+    for piece, ref in zip(piece_slices(nt_ref.shape[0]), piece_refs):
+        ref[0] = grad[piece, :]
+
+
+def qkv_weight_grads(normed_t, grads):
+    width, length = normed_t.shape
+    columns = grads.shape[2]
+    tile = min(256, columns)
+    sizes = piece_sizes(width)
+    return pl.pallas_call(
+        qkv_weight_kernel,
+        grid=(3, columns // tile),
+        in_specs=[
+            pl.BlockSpec((width, length), lambda k, u: (0, 0), pipeline_mode=pl.Buffered(1)),
+            pl.BlockSpec((1, length, tile), lambda k, u: (k, 0, u)),
+        ],
+        out_specs=[pl.BlockSpec((1, size, tile), lambda k, u: (k, 0, u)) for size in sizes],
+        out_shape=[jax.ShapeDtypeStruct((3, size, columns), BF16) for size in sizes],
+        compiler_params=pltpu.CompilerParams(vmem_limit_bytes=VMEM_BYTES),
+        cost_estimate=pl.CostEstimate(
+            flops=6 * length * width * columns,
+            bytes_accessed=2 * length * width + 12 * width * columns,
+            transcendentals=0,
+        ),
+        name="qkv_weight_grads",
+    )(normed_t, grads)
+
+
+def qkv_back_kernel(grads_ref, w_ref, out_ref, acc):
+    step = pl.program_id(0)
+    part = dot_nt(grads_ref[0], w_ref[...])
+
+    @pl.when(step == 0)
+    def _():
+        acc[...] = part
+
+    @pl.when(step > 0)
+    def _():
+        acc[...] += part
+
+    @pl.when(step == pl.num_programs(0) - 1)
+    def _():
+        out_ref[...] = acc[...].astype(BF16)
+
+
+def qkv_back(grads, weights):
+    _, length, columns = grads.shape
+    width = weights.shape[0]
+    return pl.pallas_call(
+        qkv_back_kernel,
+        grid=(3,),
+        in_specs=[
+            pl.BlockSpec((1, length, columns), lambda k: (k, 0, 0)),
+            pl.BlockSpec((width, columns), lambda k: (0, k)),
+        ],
+        out_specs=whole_spec((length, width)),
+        out_shape=jax.ShapeDtypeStruct((length, width), BF16),
+        scratch_shapes=[pltpu.VMEM((length, width), F32)],
+        compiler_params=pltpu.CompilerParams(vmem_limit_bytes=VMEM_BYTES),
+        cost_estimate=pl.CostEstimate(
+            flops=6 * length * width * columns,
+            bytes_accessed=8 * length * width,
+            transcendentals=0,
+        ),
+        name="qkv_back",
+    )(grads, weights)
+
+
+def cube_moves(sizes):
+    groups, ranks = sizes["a"], sizes["h"] * sizes["l"]
+    far = groups // 2
+    swap_to = {}
+    for group in range(2):
+        for part in range(ranks):
+            place = (part % 2) * ranks + group * (ranks // 2) + part // 2
+            swap_to[group * ranks + part] = place
+
+    def swap(values, inverse=False):
+        pairs = [(to, frm) if inverse else (frm, to) for frm, to in swap_to.items()]
+        return lax.ppermute(values, SWAP, pairs)
+
+    def hop(values, a_mask, h_mask):
+        pairs = []
+        for a in range(groups):
+            for c in range(2):
+                for h in range(2):
+                    pairs.append(((a * 2 + c) * 2 + h, ((a ^ a_mask) * 2 + c) * 2 + (h ^ h_mask)))
+        return lax.ppermute(values, CUBE, pairs)
+
+    def gather(shard):
+        shard = swap(shard)
+        near = jnp.concatenate([shard] + [hop(shard, 2 * i, 0) for i in range(1, far)], axis=0)
+        half = near.shape[0] // 2
+        by_y = hop(near, 1, 0)
+        by_x = hop(near, 0, 1)
+        return [near, by_y, by_x, hop(by_y[:half], 0, 1), hop(by_x[half:], 1, 0)]
+
+    def add(*terms):
+        total = terms[0].astype(F32)
+        for term in terms[1:]:
+            total = total + term.astype(F32)
+        return total.astype(BF16)
+
+    def scatter(pieces):
+        near, by_y, by_x, low, high = pieces
+        half = low.shape[1]
+        rows = near.shape[1] // far
+        y_high = hop(by_y[:, half:], 1, 0)
+        x_low = hop(by_x[:, :half], 0, 1)
+        low = hop(low, 0, 1)
+        high = hop(high, 1, 0)
+        y_low = hop(add(by_y[:, :half], low), 1, 0)
+        x_high = hop(add(by_x[:, half:], high), 0, 1)
+        sums = [add(near[:, :half], y_low, x_low), add(near[:, half:], y_high, x_high)]
+        total = sums[0][:, :rows].astype(F32)
+        for i in range(1, far):
+            part, place = divmod(i * rows, half)
+            total = total + hop(sums[part][:, place : place + rows], 2 * i, 0).astype(F32)
+        return swap(total.astype(BF16), inverse=True).astype(F32)
+
+    def sum_all(values):
+        for mask in range(groups.bit_length() - 1):
+            values = values + hop(values, 1 << mask, 0)
+        values = values + hop(values, 0, 1)
+        values = values + lax.ppermute(values, "c", [(0, 1), (1, 0)])
+        return lax.psum(values, "l") if sizes["l"] > 1 else values
+
+    a, h = lax.axis_index("a"), lax.axis_index("h")
+    order = []
+    for a_low, h_mask in ((0, 0), (1, 0), (0, 1), (1, 1)):
+        for i in range(far):
+            order.append((a ^ (2 * i + a_low)) * 2 + (h ^ h_mask))
+    block = jnp.arange(2 * groups)
+    a_rel, h_rel = (block // 2) ^ a, (block % 2) ^ h
+    places = (a_rel % 2 + 2 * h_rel) * far + a_rel // 2
+    return swap, gather, scatter, sum_all, jnp.stack(order), places
 
 
 def per_device(sizes, *arguments):
@@ -308,22 +560,12 @@
     ) = arguments
     ranks = sizes["h"] * sizes["l"]
     rank = lax.axis_index(TP)
-    length = segment_ids.shape[0]
-    own_rows = block_input.shape[0]
+    own_rows, width = block_input.shape
     head_width = w_query.shape[1]
     unit_width = w_up.shape[1]
     half_units = unit_width // 2
-    forth = []
-    for group in range(2):
-        for part in range(ranks):
-            forth.append((group * ranks + part, (part % 2) * ranks + group * (ranks // 2) + part // 2))
-    back = [(to, frm) for frm, to in forth]
-
-    def move_in(values):
-        return lax.ppermute(values, SWAP, forth)
-
-    def move_out(values):
-        return lax.ppermute(values, SWAP, back)
+    block_rows = w_query.shape[0]
+    swap, gather, scatter, sum_all, order, places = cube_moves(sizes)
 
     def partner(values):
         return lax.ppermute(values, "c", [(0, 1), (1, 0)])
@@ -338,10 +580,11 @@
             jnp.concatenate([theirs, values], axis=0),
         )
 
-    def tp_sum(values):
+    def tp_terms(values):
         if ranks != 2:
-            return lax.psum(values.astype(F32), TP)
-        return values.astype(F32) + partner(values).astype(F32)
+            others = lax.psum(values.astype(F32), TP) - values.astype(F32)
+            return values, others.astype(BF16)
+        return values, partner(values)
 
     def own(values):
         return lax.dynamic_slice_in_dim(values, rank * own_rows, own_rows)
@@ -352,110 +595,110 @@
         theirs = lax.dynamic_slice_in_dim(values, (1 - rank) * own_rows, own_rows)
         return own(values).astype(F32) + partner(theirs).astype(F32)
 
-    def gather_weights(values):
-        return lax.all_gather(move_in(values), DATA, axis=0, tiled=True)
-
-    full_attn = gather_weights(jnp.concatenate([w_query, w_key, w_value, w_out], axis=1))
-    full_mlp = [
-        gather_weights(
+    def permuted(vectors):
+        stacked = jnp.stack(vectors).reshape(len(vectors), -1, block_rows)
+        return jnp.take(stacked, order, axis=1).reshape(len(vectors), width)
+
+    def restored(vectors):
+        stacked = vectors.reshape(vectors.shape[0], -1, block_rows)
+        return jnp.take(stacked, places, axis=1).reshape(vectors.shape)
+
+    sources = jnp.repeat(order, block_rows) * block_rows + jnp.arange(width) % block_rows
+    shuffle = (jnp.arange(width)[:, None] == sources[None, :]).astype(BF16)
+
+    pieces_qkv = gather(jnp.concatenate([w_query, w_key, w_value], axis=1))
+    pieces_out = gather(w_out)
+    pieces_mlp = [
+        gather(
             jnp.concatenate(
                 [w_up[:, first : first + half_units], w_down[:, first : first + half_units]], axis=1
             )
         )
         for first in (0, half_units)
     ]
-    full_qkv = full_attn[:, : 3 * head_width]
-    full_out = full_attn[:, 3 * head_width :]
-    own_input = move_in(block_input)
-    segments = move_in(segment_ids)
-    own_grad = move_in(out_grad)
+    gain_one, bias_one, gain_two, bias_two, shift_out, shift_down = permuted(
+        [ln1_gain, ln1_bias, ln2_gain, ln2_bias, b_out, b_down]
+    )
+    own_input = dot_nn(swap(block_input), shuffle).astype(BF16)
+    segments = swap(segment_ids)
+    own_grad = dot_nn(swap(out_grad), shuffle).astype(BF16)
     bias_query = lax.dynamic_slice_in_dim(b_query, rank * head_width, head_width)
     bias_value = lax.dynamic_slice_in_dim(b_value, rank * head_width, head_width)
     bias_up = lax.dynamic_slice_in_dim(b_up, rank * unit_width, unit_width)
 
-    rows_in = tp_gather(own_input).astype(F32)
+    rows_in = tp_gather(own_input)
     grad_rows = tp_gather(own_grad)
-    scaled_one, _ = normalize(rows_in)
-    normed = (scaled_one * ln1_gain + ln1_bias).astype(BF16)
+    grad_rows_t = grad_rows.T
+    normed, normed_t = norm_rows(rows_in, gain_one, bias_one)
     scale = HEAD_DIM ** (-0.5)
     factors = jnp.concatenate([jnp.full((head_width,), scale, F32), jnp.ones((2 * head_width,), F32)])
     biases = jnp.concatenate([bias_query * scale, jnp.zeros((head_width,), F32), bias_value])
+    full_qkv = jnp.concatenate(pieces_qkv, axis=0)
+    full_out = jnp.concatenate(pieces_out, axis=0)
     qkv = (dot_nn(normed, full_qkv) * factors + biases).astype(BF16)
     mixed, lse = attn_forward(segments, qkv, head_width)
-    attended = tp_sum(dot_nt(mixed, full_out).astype(BF16))
-    hidden = rows_in + attended + b_out
-    scaled_two, inverse_two = normalize(hidden)
-    normed_two = (scaled_two * ln2_gain + ln2_bias).astype(BF16)
-    normed_two_t = normed_two.T
-    grad_rows_t = grad_rows.T
-
-    out_parts, gn_parts, up_parts, down_parts, bias_parts = [], [], [], [], []
+    attended = tp_terms(dot_nt(mixed, full_out).astype(BF16))
+    normed_two, normed_two_t, hidden = norm_rows(rows_in, gain_two, bias_two, attended, shift_out)
+
+    previous, mlp_grads, bias_parts = (), [], []
     for index, first in enumerate((0, half_units)):
-        results = mlp(
-            normed_two, grad_rows, normed_two_t, grad_rows_t, full_mlp[index],
-            bias_up[first : first + half_units],
+        out_part, gn_part, grad_pieces, bias_part = mlp(
+            normed_two, grad_rows, normed_two_t, grad_rows_t, pieces_mlp[index],
+            bias_up[first : first + half_units], previous,
         )
-        for values, store in zip(results, (out_parts, gn_parts, up_parts, down_parts, bias_parts)):
-            store.append(values)
-    gn_part = (gn_parts[0].astype(F32) + gn_parts[1].astype(F32)).astype(BF16)
-    out_part = (out_parts[0].astype(F32) + out_parts[1].astype(F32)).astype(BF16)
-    output = move_out((own(hidden) + tp_scatter(out_part) + b_down).astype(BF16))
-
-    grad_normed_two = tp_sum(gn_part)
-    grad_hidden = grad_rows.astype(F32) + norm_back(grad_normed_two, scaled_two, inverse_two, ln2_gain)
-    grad_attended = grad_hidden.astype(BF16)
+        previous = (out_part, gn_part)
+        mlp_grads.append(scatter(grad_pieces))
+        bias_parts.append(bias_part[0])
+    own_output = (own(hidden) + tp_scatter(out_part) + shift_down).astype(BF16)
+    output = swap(dot_nt(own_output, shuffle).astype(BF16), inverse=True)
+
+    grad_hidden, grad_attended, sums_two = norm_back_rows(
+        hidden, grad_rows, tp_terms(gn_part), gain_two
+    )
     grad_mixed = dot_nn(grad_attended, full_out).astype(BF16)
     grad_out_part = dot_tn(grad_attended, mixed).astype(BF16)
-
-    def scatter_weights(values):
-        return move_out(lax.psum_scatter(values, DATA, scatter_dimension=0, tiled=True)).astype(F32)
-
-    early = scatter_weights(jnp.concatenate(up_parts + down_parts + [grad_out_part], axis=1))
-    grad_w_up = early[:, :unit_width]
-    grad_w_down = early[:, unit_width : 2 * unit_width]
-    grad_w_out = early[:, 2 * unit_width :]
+    grad_w_out = scatter([grad_out_part[None, piece] for piece in piece_slices(width)])[0]
 
     grads = attn_backward(segments, qkv, mixed, lse, grad_mixed, head_width)
-    late = scatter_weights(
-        jnp.concatenate([dot_tn(normed, grads[place]).astype(BF16) for place in range(3)], axis=1)
-    )
-    grad_normed_part = (
-        dot_nt(grads[0], full_qkv[:, :head_width])
-        + dot_nt(grads[1], full_qkv[:, head_width : 2 * head_width])
-        + dot_nt(grads[2], full_qkv[:, 2 * head_width :])
-    ).astype(BF16)
-    grad_normed = tp_scatter(grad_normed_part)
+    late = scatter(qkv_weight_grads(normed_t, grads))
+    grad_normed = tp_scatter(qkv_back(grads, full_qkv))
     own_scaled, own_inverse = normalize(own_input.astype(F32))
-    grad_own = own(grad_hidden) + norm_back(grad_normed, own_scaled, own_inverse, ln1_gain)
-    grad_input = move_out(grad_own.astype(BF16))
+    grad_own = own(grad_hidden) + norm_back(grad_normed, own_scaled, own_inverse, gain_one)
+    grad_input = swap(dot_nt(grad_own.astype(BF16), shuffle).astype(BF16), inverse=True)
 
     def place_part(values, full):
         return lax.dynamic_update_slice_in_dim(
             jnp.zeros((full,), F32), values, rank * values.shape[0], 0
         )
 
-    width = ln1_gain.shape[0]
-    share = 1.0 / ranks
-    sums = jnp.concatenate(
+    early = jnp.concatenate(
         [
-            jnp.sum(grad_normed * own_scaled, axis=0),
-            jnp.sum(grad_normed, axis=0),
+            restored(
+                jnp.concatenate(
+                    [sums_two[:3] * (1.0 / ranks), jnp.sum(own_grad.astype(F32), axis=0)[None]], axis=0
+                )
+            ).reshape(-1),
+            place_part(jnp.concatenate(bias_parts), b_up.shape[0]),
+        ]
+    )
+    early = sum_all(early)
+    last = jnp.concatenate(
+        [
+            restored(
+                jnp.stack([jnp.sum(grad_normed * own_scaled, axis=0), jnp.sum(grad_normed, axis=0)])
+            ).reshape(-1),
             place_part(jnp.sum(grads[0].astype(F32), axis=0), width),
             place_part(jnp.sum(grads[2].astype(F32), axis=0), width),
-            jnp.sum(grad_hidden, axis=0) * share,
-            jnp.sum(grad_normed_two * scaled_two, axis=0) * share,
-            jnp.sum(grad_normed_two, axis=0) * share,
-            jnp.sum(own_grad.astype(F32), axis=0),
-            place_part(jnp.concatenate(bias_parts, axis=1)[0], b_up.shape[0]),
         ]
     )
-    sums = lax.psum(sums, ("a", "c", "h", "l"))
-    small = [sums[place * width : (place + 1) * width] for place in range(8)]
+    last = sum_all(last)
+    early_rows = [early[i * width : (i + 1) * width] for i in range(4)]
+    last_rows = [last[i * width : (i + 1) * width] for i in range(4)]
     return (
-        output, grad_input, small[0], small[1],
-        late[:, :head_width], late[:, head_width : 2 * head_width], late[:, 2 * head_width :],
-        small[2], small[3], grad_w_out, small[4], small[5], small[6], grad_w_up,
-        sums[8 * width :], grad_w_down, small[7],
+        output, grad_input, last_rows[0], last_rows[1], late[0], late[1], late[2],
+        last_rows[2], last_rows[3], grad_w_out, early_rows[0], early_rows[1], early_rows[2],
+        jnp.concatenate([part[0] for part in mlp_grads], axis=1), early[4 * width :],
+        jnp.concatenate([part[1] for part in mlp_grads], axis=1), early_rows[3],
     )
 
 

time: 640 us -> 549 us (0.86)
  waiting for transfers between devices: 331 us -> 160 us
  starting transfers between devices: 24.8 us -> 135 us
  blocking collectives: 43.7 us -> 0 us
  Pallas kernels: 89.6 us -> 128 us
  between operations: 15 us -> 2.21 us
  other arithmetic: 40.1 us -> 32.9 us
    ppermute x10 -> x87, waiting for transfers between devices: 31.8 us -> 159 us  [the longest x72 157 us: hop(): return lax.ppermute(values, CUBE, pairs)]
    ppermute x10 -> x87, starting transfers between devices: 22.7 us -> 133 us  [the longest x72 92.2 us: hop(): return lax.ppermute(values, CUBE, pairs)]
    all_gather x3 -> x0, waiting for transfers between devices: 108 us -> none  [gather_weights(): return lax.all_gather(move_in(values), DATA, axis=0, tiled=True)]
    reduce_scatter x1 -> x0, waiting for transfers between devices: 96.2 us -> none  [scatter_weights(): lax.psum_scatter(values, DATA, scatter_dimension=0, tiled=True)]
    unnamed x6 -> x0, waiting for transfers between devices: 89.9 us -> none
    psum x1 -> x0, blocking collectives: 43.7 us -> none  [per_device(): sums = lax.psum(sums, ('a', 'c', 'h', 'l'))]
    pallas_call x2 -> x7, Pallas kernels: 48.9 us -> 87.6 us  [the longest x2 50.8 us: mlp(): pl.pallas_call(functools.partial(mlp_kernel, block=min(256, length), with...]
    pallas_call x4 -> x0, local copies, waits for them, and re-layouts: 14 us -> none  [mlp(): pl.pallas_call(functools.partial(mlp_kernel, block=min(256, length)), gri...]
  transfers between devices with their start and end apart: 21 -> 93, of which waited for: 12 -> 34; matrix products, arithmetic and copies ran while one was open for 16% -> 19% of each run, Pallas kernels for 10% -> 24%
where the time goes in v2:
time: 549 us; the launch traced here: 539 us
  waiting for transfers between devices  160 us (29%)
  starting transfers between devices  135 us (25%)
  Pallas kernels  128 us (23%)
  local copies, waits for them, and re-layouts  52 us (9%)
  other arithmetic  32.9 us (6%)
  matrix products  29 us (5%)
    ppermute x72, waiting for transfers between devices, hop(): return lax.ppermute(values, CUBE, pairs)  157 us
    ppermute x72, starting transfers between devices, hop(): return lax.ppermute(values, CUBE, pairs)  92.2 us
    pallas_call x2, Pallas kernels, mlp(): pl.pallas_call(functools.partial(mlp_kernel, block=min(256, length), with...  50.8 us
    ppermute x13, starting transfers between devices, swap(): return lax.ppermute(values, SWAP, pairs)  38.9 us
    pallas_call x1, Pallas kernels, attn_backward(): pl.pallas_call(functools.partial(attn_backward_kernel, block=block), grid...  24 us
    pallas_call x1, Pallas kernels, attn_forward(): pl.pallas_call(functools.partial(attn_forward_kernel, block=block), grid=...  16.4 us
    dot_general x4, matrix products, dot_nn(): lax.dot_general(left, right, (((1,), (0,)), ((), ())), preferred_element_...  15 us
    unnamed x118, local copies, waits for them, and re-layouts  14.3 us
  transfers between devices with their start and end apart: 93, of which 34 were waited for; matrix products, arithmetic and copies ran while one was open for 19% of the time, Pallas kernels for 24%

profile of v2, /device:TPU:10, one launch (start us, length us, event | category | flops | bytes accessed | tf_op | source)
XLA Modules:
  0.0 538.7 jit_solution(13511236395738442956)
XLA Ops:
  3.7 3.6 collective-permute-start.3
  9.3 3.6 collective-permute-start.11
  19.5 3.6 collective-permute-start.22
  24.6 3.8 collective-permute-done.12
  31.1 3.2 collective-permute-done.13
  40.2 3.8 collective-permute-start.4
  48.0 3.7 collective-permute-start.31
  52.3 3.2 collective-permute-start.32
  55.6 3.5 collective-permute-done.5
  59.6 13.9 %collective-permute-done.6 = bf16[64,1536]{1,0:T(8,128)(2,1)S(1)} collective-permute-done((bf16[64,1536]{1,0:T(8,128)(2,1)S(1)}, bf16[64,1536]{1,0:T(8,128)(2,1)S(1)}, u32[]{:S(2)}, u32[]{:S(2)}) %collective-permute-start.6) | collective-permute-done | bytes 196640 | tf_op jit(solution)/shard_map/ppermute | solution.py:505
  74.7 5.2 collective-permute-done.32
  81.0 2.8 collective-permute-done.33
  97.1 5.5 %collective-permute-start.9 = (bf16[128,1536]{1,0:T(8,128)(2,1)S(1)}, bf16[128,1536]{1,0:T(8,128)(2,1)S(1)}, u32[]{:S(2)}, u32[]{:S(2)}) collective-permute-start(bf16[128,1536]{1,0:T(8,128)(2,1)S(1)} %slice.324), channel_id=1, source_target_pairs={{0,1},{1,0},{2,3},{3,2},{4,5},{5,4},{6,7},{7,6},{8,9},{9,8},{10,11... | collective-permute-start | bytes 1179656 | tf_op jit(solution)/shard_map/ppermute | solution.py:505
  105.0 13.7 %collective-permute-done.9 = bf16[128,1536]{1,0:T(8,128)(2,1)S(1)} collective-permute-done((bf16[128,1536]{1,0:T(8,128)(2,1)S(1)}, bf16[128,1536]{1,0:T(8,128)(2,1)S(1)}, u32[]{:S(2)}, u32[]{:S(2)}) %collective-permute-start.9) | collective-permute-done | bytes 393248 | tf_op jit(solution)/shard_map/ppermute | solution.py:505
  127.0 5.2 norm_one.1
  132.1 7.6 %add_convert_fusion.q_ref.k_ref.v_ref = bf16[1024,1536]{1,0:T(8,128)(2,1)} fusion(bf16[1024,1024]{1,0:T(8,128)(2,1)} %get-tuple-element.48, bf16[1024,1536]{1,0:T(8,128)(2,1)} %copy-done.27, f32[1536]{0:T(1024)S(1)} %pad_maximum_fusion.9, f32[1536]{0:T(1024)S(1)} %copy-done.48), kind=kOutput, calls=%fused_computation.3 | convolution fusion | flops 3225944064 | bytes 8400896 | tf_op jit(solution)/shard_map/dot_general | solution.py:39
  139.7 16.4 %attn_forward.1 = (bf16[1024,512]{1,0:T(8,128)(2,1)}, f32[4,8,1024]{2,1,0:T(8,128)}) custom-call(s32[1024,1]{1,0:T(8,128)} %copy.46.seg_col, s32[1,1024]{1,0:T(1,128)} %bitcast.94, bf16[1024,1536]{1,0:T(8,128)(2,1)} %add_convert_fusion.q_ref.k_ref.v_ref, bf16[1024,1536]{1,0:T(8,128)(2,1)} %add_convert_fusion.q_ref.k_ref.v_ref, ...), custom_call_target="tpu_custom_call" | custom-call | flops 2147483648 | bytes 4194304 | tf_op jit(solution)/shard_map/attn_forward/pallas_call | solution.py:155
  156.1 4.2 convolution_convert_fusion.refs_1_
  175.5 12.1 %collective-permute-done.26.refs_1_.refs_6_ = bf16[256,2048]{1,0:T(8,128)(2,1)} collective-permute-done((bf16[256,2048]{1,0:T(8,128)(2,1)}, bf16[256,2048]{1,0:T(8,128)(2,1)}, u32[]{:S(2)}, u32[]{:S(2)}) %collective-permute-start.26) | collective-permute-done | bytes 1048608 | tf_op jit(solution)/shard_map/ppermute | solution.py:505
  195.6 3.4 maximum_select_fusion.1.g_ref
  201.7 7.3 %norm_two.1 = (bf16[1024,1024]{1,0:T(8,128)(2,1)}, bf16[1024,1024]{1,0:T(8,128)(2,1)}, f32[1024,1024]{1,0:T(8,128)}) custom-call(bf16[1024,1024]{1,0:T(8,128)(2,1)} %maximum_select_fusion.refs_0_, bf16[1024,1024]{1,0:T(8,128)(2,1)} %convolution_convert_fusion.refs_1_, bf16[1024,1024]{1,0:T(8,128)(2,1)} %collective-permute-done.19.refs_2_, ...), custom_call_target="tpu_custom_call" | custom-call | flops 20971520 | bytes 14680064 | tf_op jit(solution)/shard_map/norm_two/pallas_call | solution.py:258
  209.0 25.0 %mlp_both.2 = (bf16[1024,1024]{1,0:T(8,128)(2,1)}, bf16[1024,1024]{1,0:T(8,128)(2,1)}, bf16[2,256,1024]{2,1,0:T(8,128)(2,1)}, bf16[2,256,1024]{2,1,0:T(8,128)(2,...) custom-call(bf16[1024,1024]{1,0:T(8,128)(2,1)} %get-tuple-element.51, ...), custom_call_target="tpu_custom_call" | custom-call | flops 12884901888 | bytes 20971520 | tf_op jit(solution)/shard_map/mlp_both/pallas_call | solution.py:378
  240.5 25.8 %mlp_both.3 = (bf16[1024,1024]{1,0:T(8,128)(2,1)}, bf16[1024,1024]{1,0:T(8,128)(2,1)}, bf16[2,256,1024]{2,1,0:T(8,128)(2,1)}, bf16[2,256,1024]{2,1,0:T(8,128)(2,...) custom-call(bf16[1024,1024]{1,0:T(8,128)(2,1)} %get-tuple-element.51, ...), custom_call_target="tpu_custom_call" | custom-call | flops 12884901888 | bytes 20971520 | tf_op jit(solution)/shard_map/mlp_both/pallas_call | solution.py:378
  272.7 5.9 %collective-permute-done.88 = bf16[2,128,1024]{2,1,0:T(8,128)(2,1)S(1)} collective-permute-done((bf16[2,128,1024]{2,1,0:T(8,128)(2,1)}, bf16[2,128,1024]{2,1,0:T(8,128)(2,1)S(1)}, u32[]{:S(2)}, u32[]{:S(2)}) %collective-permute-start.88) | collective-permute-done | bytes 524320 | tf_op jit(solution)/shard_map/ppermute | solution.py:505
  280.2 4.9 collective-permute-done.83
  287.8 8.5 %collective-permute-done.79 = bf16[2,128,1024]{2,1,0:T(8,128)(2,1)S(1)} collective-permute-done((bf16[2,128,1024]{2,1,0:T(8,128)(2,1)S(1)}, bf16[2,128,1024]{2,1,0:T(8,128)(2,1)S(1)}, u32[]{:S(2)}, u32[]{:S(2)}) %collective-permute-start.79) | collective-permute-done | bytes 524320 | tf_op jit(solution)/shard_map/ppermute | solution.py:505
  300.6 6.9 %collective-permute-done.85 = bf16[2,128,1024]{2,1,0:T(8,128)(2,1)S(1)} collective-permute-done((bf16[2,128,1024]{2,1,0:T(8,128)(2,1)S(1)}, bf16[2,128,1024]{2,1,0:T(8,128)(2,1)S(1)}, u32[]{:S(2)}, u32[]{:S(2)}) %collective-permute-start.85) | collective-permute-done | bytes 524320 | tf_op jit(solution)/shard_map/ppermute | solution.py:505
  307.5 7.7 %collective-permute-done.89 = bf16[2,128,1024]{2,1,0:T(8,128)(2,1)S(1)} collective-permute-done((bf16[2,128,1024]{2,1,0:T(8,128)(2,1)S(1)}, bf16[2,128,1024]{2,1,0:T(8,128)(2,1)S(1)}, u32[]{:S(2)}, u32[]{:S(2)}) %collective-permute-start.89) | collective-permute-done | bytes 524320 | tf_op jit(solution)/shard_map/ppermute | solution.py:505
  317.2 8.3 %collective-permute-done.80 = bf16[2,64,1024]{2,1,0:T(8,128)(2,1)S(1)} collective-permute-done((bf16[2,64,1024]{2,1,0:T(8,128)(2,1)S(1)}, bf16[2,64,1024]{2,1,0:T(8,128)(2,1)S(1)}, u32[]{:S(2)}, u32[]{:S(2)}) %collective-permute-start.80) | collective-permute-done | bytes 262176 | tf_op jit(solution)/shard_map/ppermute | solution.py:505
  325.5 3.4 collective-permute-start.90
  328.9 15.1 %collective-permute-done.81 = bf16[2,64,1024]{2,1,0:T(8,128)(2,1)S(1)} collective-permute-done((bf16[2,64,1024]{2,1,0:T(8,128)(2,1)S(1)}, bf16[2,64,1024]{2,1,0:T(8,128)(2,1)S(1)}, u32[]{:S(2)}, u32[]{:S(2)}) %collective-permute-start.81) | collective-permute-done | bytes 262176 | tf_op jit(solution)/shard_map/ppermute | solution.py:505
  345.1 3.0 collective-permute-done.90
  348.0 3.0 collective-permute-start.82
  351.1 4.1 collective-permute-done.91
  355.3 3.2 collective-permute-start.92
  365.3 8.5 %norm_two_back.1 = (f32[1024,1024]{1,0:T(8,128)}, bf16[1024,1024]{1,0:T(8,128)(2,1)}, f32[8,1024]{1,0:T(8,128)}) custom-call(f32[1024,1024]{1,0:T(8,128)} %get-tuple-element.50.hidden_ref, bf16[1024,1024]{1,0:T(8,128)(2,1)} %copy-done, bf16[1024,1024]{1,0:T(8,128)(2,1)} %get-tuple-element.56.own_ref, bf16[1024,1024]{1,0:T(8,128)(2,1)} %collective-permute-done.40.other_ref, ...), custom_call_target="tpu_custom_call" | custom-call | flops 31457280 | bytes 16777216 | tf_op jit(solution)/shard_map/norm_two_back/pallas_call | solution.py:297
  373.9 3.3 convolution_convert_fusion.1
  381.1 24.0 %attn_backward.1.grads_ref = bf16[3,1024,512]{2,1,0:T(8,128)(2,1)} custom-call(s32[1024,1]{1,0:T(8,128)} %copy.46.seg_col, s32[1,1024]{1,0:T(1,128)} %bitcast.95, bf16[1024,1536]{1,0:T(8,128)(2,1)} %add_convert_fusion.q_ref.k_ref.v_ref, bf16[1024,1536]{1,0:T(8,128)(2,1)} %add_convert_fusion.q_ref.k_ref.v_ref, ...), custom_call_target="tpu_custom_call" | custom-call | flops 5368709120 | bytes 8388608 | tf_op jit(solution)/shard_map/attn_backward/pallas_call | solution.py:184
  405.2 7.9 %qkv_back.1 = bf16[1024,1024]{1,0:T(8,128)(2,1)} custom-call(bf16[3,1024,512]{2,1,0:T(8,128)(2,1)} %attn_backward.1.grads_ref, bf16[1024,1536]{1,0:T(8,128)(2,1)} %copy-done.27), custom_call_target="tpu_custom_call" | custom-call | flops 3221225472 | bytes 8388608 | tf_op jit(solution)/shard_map/qkv_back/pallas_call | solution.py:466
  422.5 6.4 %collective-permute-start.58 = (bf16[1,128,512]{2,1,0:T(8,128)(2,1)}, bf16[1,128,512]{2,1,0:T(8,128)(2,1)}, u32[]{:S(2)}, u32[]{:S(2)}) collective-permute-start(bf16[1,128,512]{2,1,0:T(8,128)(2,1)} %get-tuple-element.95), channel_id=1, source_target_pairs={{0,1},{1,0},{2,3},{3,2},{4,5},{5,4},{6,7},{7,6},{8,9},{9,8},{10,11... | collective-permute-start | bytes 393224 | tf_op jit(solution)/shard_map/ppermute | solution.py:505
  432.3 7.9 %qkv_weight_grads.1 = (bf16[3,256,512]{2,1,0:T(8,128)(2,1)}, bf16[3,256,512]{2,1,0:T(8,128)(2,1)}, bf16[3,256,512]{2,1,0:T(8,128)(2,1)}, bf16[3,128,512]{2,1,0:T(8,128)(2,1)}, bf16[3,128,512]{2,1,0:T(8,128)(2,1)}) custom-call(bf16[1024,1024]{1,0:T(8,128)(2,1)} %get-tuple-element.60.nt_ref, bf16[3,1024,512]{2,1,0:T(8,128)(2,1)} %attn_backward.1.grads_ref), custom_call_target="tpu_custom_call" | custom-call | flops 3221225472 | bytes 8388608 | tf_op jit(solution)/shard_map/qkv_weight_grads/pallas_call | solution.py:427
  458.6 4.7 collective-permute-done.53
  476.5 2.9 collective-permute-done.52
  479.4 3.3 collective-permute-done.54
  482.7 3.0 collective-permute-done.49
  500.8 4.0 fusion.26
  515.1 4.2 collective-permute-done.46
  523.3 7.7 %collective-permute-start.57 = (bf16[3,64,512]{2,1,0:T(8,128)(2,1)S(1)}, bf16[3,64,512]{2,1,0:T(8,128)(2,1)S(1)}, u32[]{:S(2)}, u32[]{:S(2)}) collective-permute-start(bf16[3,64,512]{2,1,0:T(8,128)(2,1)S(1)} %add_convert_fusion.17), channel_id=1, source_target_pairs={{0,0},{2,1},{1,2},{3,3},{4,4},{6,5},{5,6},{7,7},{8,8},{10,9},{9,10... | collective-permute-start | bytes 589832 | tf_op jit(solution)/shard_map/ppermute | solution.py:497
  (416 shorter events, 194.4 us)
Async XLA Ops:
  0.7 87.7 %collective-permute-start = (bf16[512,1024]{1,0:T(8,128)(2,1)}, bf16[512,1024]{1,0:T(8,128)(2,1)}, u32[]{:S(2)}, u32[]{:S(2)}) collective-permute-start(bf16[512,1024]{1,0:T(8,128)(2,1)} %param.18), channel_id=1, source_target_pairs={{0,0},{1,2},{2,1},{3,3},{4,4},{5,6},{6,5},{7,7},{8,8},{9,10},{10,9... | collective-permute-start | bytes 3145736 | tf_op jit(solution)/shard_map/ppermute | solution.py:497
  3.7 36.4 %collective-permute-start.3 = (bf16[64,1536]{1,0:T(8,128)(2,1)S(1)}, bf16[64,1536]{1,0:T(8,128)(2,1)S(1)}, u32[]{:S(2)}, u32[]{:S(2)}) collective-permute-start(bf16[64,1536]{1,0:T(8,128)(2,1)S(1)} %pad_maximum_fusion.4), channel_id=1, source_target_pairs={{0,0},{1,2},{2,1},{3,3},{4,4},{5,6},{6,5},{7,7},{8,8},{9,10},{10,9... | collective-permute-start | bytes 589832 | tf_op jit(solution)/shard_map/ppermute | solution.py:497
  14.1 26.0 %collective-permute-start.30 = (bf16[64,2048]{1,0:T(8,128)(2,1)S(1)}, bf16[64,2048]{1,0:T(8,128)(2,1)S(1)}, u32[]{:S(2)}, u32[]{:S(2)}) collective-permute-start(bf16[64,2048]{1,0:T(8,128)(2,1)S(1)} %pad_maximum_fusion.3), channel_id=1, source_target_pairs={{0,0},{1,2},{2,1},{3,3},{4,4},{5,6},{6,5},{7,7},{8,8},{9,10},{10,9... | collective-permute-start | bytes 786440 | tf_op jit(solution)/shard_map/ppermute | solution.py:497
  19.5 25.2 %collective-permute-start.22 = (bf16[64,2048]{1,0:T(8,128)(2,1)S(1)}, bf16[64,2048]{1,0:T(8,128)(2,1)S(1)}, u32[]{:S(2)}, u32[]{:S(2)}) collective-permute-start(bf16[64,2048]{1,0:T(8,128)(2,1)S(1)} %pad_maximum_fusion.2), channel_id=1, source_target_pairs={{0,0},{1,2},{2,1},{3,3},{4,4},{5,6},{6,5},{7,7},{8,8},{9,10},{10,9... | collective-permute-start | bytes 786440 | tf_op jit(solution)/shard_map/ppermute | solution.py:497
  47.4 26.2 %collective-permute-start.6 = (bf16[64,1536]{1,0:T(8,128)(2,1)S(1)}, bf16[64,1536]{1,0:T(8,128)(2,1)S(1)}, u32[]{:S(2)}, u32[]{:S(2)}) collective-permute-start(bf16[64,1536]{1,0:T(8,128)(2,1)S(1)} %collective-permute-done.3), channel_id=1, source_target_pairs={{0,24},{1,25},{2,26},{3,27},{4,28},{5,29},{6,30},{7,31},{8,16},{9,... | collective-permute-start | bytes 589832 | tf_op jit(solution)/shard_map/ppermute | solution.py:505
  48.0 25.6 %collective-permute-start.31 = (bf16[64,2048]{1,0:T(8,128)(2,1)S(1)}, bf16[64,2048]{1,0:T(8,128)(2,1)S(1)}, u32[]{:S(2)}, u32[]{:S(2)}) collective-permute-start(bf16[64,2048]{1,0:T(8,128)(2,1)S(1)} %collective-permute-done.30), channel_id=1, source_target_pairs={{0,8},{1,9},{2,10},{3,11},{4,12},{5,13},{6,14},{7,15},{8,0},{9,1},... | collective-permute-start | bytes 786440 | tf_op jit(solution)/shard_map/ppermute | solution.py:505
  52.3 27.6 %collective-permute-start.32 = (bf16[64,2048]{1,0:T(8,128)(2,1)S(1)}, bf16[64,2048]{1,0:T(8,128)(2,1)S(1)}, u32[]{:S(2)}, u32[]{:S(2)}) collective-permute-start(bf16[64,2048]{1,0:T(8,128)(2,1)S(1)} %collective-permute-done.30), channel_id=1, source_target_pairs={{0,16},{1,17},{2,18},{3,19},{4,20},{5,21},{6,22},{7,23},{8,24},{9,... | collective-permute-start | bytes 786440 | tf_op jit(solution)/shard_map/ppermute | solution.py:505
  59.1 24.7 %collective-permute-start.33 = (bf16[64,2048]{1,0:T(8,128)(2,1)S(1)}, bf16[64,2048]{1,0:T(8,128)(2,1)S(1)}, u32[]{:S(2)}, u32[]{:S(2)}) collective-permute-start(bf16[64,2048]{1,0:T(8,128)(2,1)S(1)} %collective-permute-done.30), channel_id=1, source_target_pairs={{0,24},{1,25},{2,26},{3,27},{4,28},{5,29},{6,30},{7,31},{8,16},{9,... | collective-permute-start | bytes 786440 | tf_op jit(solution)/shard_map/ppermute | solution.py:505
  83.8 20.5 %collective-permute-start.8 = (bf16[256,1536]{1,0:T(8,128)(2,1)S(1)}, bf16[256,1536]{1,0:T(8,128)(2,1)S(1)}, u32[]{:S(2)}, u32[]{:S(2)}) collective-permute-start(bf16[256,1536]{1,0:T(8,128)(2,1)S(1)} %get-tuple-element.121), channel_id=1, source_target_pairs={{0,1},{1,0},{2,3},{3,2},{4,5},{5,4},{6,7},{7,6},{8,9},{9,8},{10,11... | collective-permute-start | bytes 2359304 | tf_op jit(solution)/shard_map/ppermute | solution.py:505
  84.8 78.3 %collective-permute-start.20 = (bf16[512,1024]{1,0:T(8,128)(2,1)}, bf16[512,1024]{1,0:T(8,128)(2,1)}, u32[]{:S(2)}, u32[]{:S(2)}) collective-permute-start(bf16[512,1024]{1,0:T(8,128)(2,1)} %param.35), channel_id=1, source_target_pairs={{0,0},{1,2},{2,1},{3,3},{4,4},{5,6},{6,5},{7,7},{8,8},{9,10},{10,9... | collective-permute-start | bytes 3145736 | tf_op jit(solution)/shard_map/ppermute | solution.py:497
  86.7 73.5 %collective-permute-start.24 = (bf16[64,2048]{1,0:T(8,128)(2,1)S(1)}, bf16[64,2048]{1,0:T(8,128)(2,1)S(1)}, u32[]{:S(2)}, u32[]{:S(2)}) collective-permute-start(bf16[64,2048]{1,0:T(8,128)(2,1)S(1)} %collective-permute-done.22), channel_id=1, source_target_pairs={{0,16},{1,17},{2,18},{3,19},{4,20},{5,21},{6,22},{7,23},{8,24},{9,... | collective-permute-start | bytes 786440 | tf_op jit(solution)/shard_map/ppermute | solution.py:505
  95.0 25.4 %collective-permute-start.1 = (bf16[512,1024]{1,0:T(8,128)(2,1)S(1)}, bf16[512,1024]{1,0:T(8,128)(2,1)S(1)}, u32[]{:S(2)}, u32[]{:S(2)}) collective-permute-start(bf16[512,1024]{1,0:T(8,128)(2,1)S(1)} %get-tuple-element.151), channel_id=1, source_target_pairs={{0,2},{2,0},{1,3},{3,1},{4,6},{6,4},{5,7},{7,5},{8,10},{10,8},{9,1... | collective-permute-start | bytes 3145736 | tf_op jit(solution)/shard_map/ppermute | solution.py:571
  97.1 21.6 %collective-permute-start.9 = (bf16[128,1536]{1,0:T(8,128)(2,1)S(1)}, bf16[128,1536]{1,0:T(8,128)(2,1)S(1)}, u32[]{:S(2)}, u32[]{:S(2)}) collective-permute-start(bf16[128,1536]{1,0:T(8,128)(2,1)S(1)} %slice.324), channel_id=1, source_target_pairs={{0,1},{1,0},{2,3},{3,2},{4,5},{5,4},{6,7},{7,6},{8,9},{9,8},{10,11... | collective-permute-start | bytes 1179656 | tf_op jit(solution)/shard_map/ppermute | solution.py:505
  118.7 42.3 %collective-permute-start.25 = (bf16[64,2048]{1,0:T(8,128)(2,1)S(1)}, bf16[64,2048]{1,0:T(8,128)(2,1)S(1)}, u32[]{:S(2)}, u32[]{:S(2)}) collective-permute-start(bf16[64,2048]{1,0:T(8,128)(2,1)S(1)} %collective-permute-done.22), channel_id=1, source_target_pairs={{0,24},{1,25},{2,26},{3,27},{4,28},{5,29},{6,30},{7,31},{8,16},{9,... | collective-permute-start | bytes 786440 | tf_op jit(solution)/shard_map/ppermute | solution.py:505
  119.6 46.8 %collective-permute-start.34 = (bf16[256,2048]{1,0:T(8,128)(2,1)}, bf16[256,2048]{1,0:T(8,128)(2,1)S(1)}, u32[]{:S(2)}, u32[]{:S(2)}) collective-permute-start(bf16[256,2048]{1,0:T(8,128)(2,1)} %constant_dynamic-update-slice_fusion.28.refs_0_.refs_5_), channel_id=1, source_target_pairs={{0,4},{1,5},{2,6},{3,7},{4,0},{5,1},{6,2},{7,3},{8,12},{9,13},{10,... | collective-permute-start | bytes 3145736 | tf_op jit(solution)/shard_map/ppermute | solution.py:505
  122.1 50.2 %collective-permute-start.35 = (bf16[256,2048]{1,0:T(8,128)(2,1)}, bf16[256,2048]{1,0:T(8,128)(2,1)}, u32[]{:S(2)}, u32[]{:S(2)}) collective-permute-start(bf16[256,2048]{1,0:T(8,128)(2,1)} %constant_dynamic-update-slice_fusion.28.refs_0_.refs_5_), channel_id=1, source_target_pairs={{0,1},{1,0},{2,3},{3,2},{4,5},{5,4},{6,7},{7,6},{8,9},{9,8},{10,11... | collective-permute-start | bytes 3145736 | tf_op jit(solution)/shard_map/ppermute | solution.py:505
  160.3 41.5 %collective-permute-start.19 = (bf16[1024,1024]{1,0:T(8,128)(2,1)}, bf16[1024,1024]{1,0:T(8,128)(2,1)}, u32[]{:S(2)}, u32[]{:S(2)}) collective-permute-start(bf16[1024,1024]{1,0:T(8,128)(2,1)} %convolution_convert_fusion.refs_1_), channel_id=1, source_target_pairs={{0,2},{2,0},{1,3},{3,1},{4,6},{6,4},{5,7},{7,5},{8,10},{10,8},{9,1... | collective-permute-start | bytes 6291464 | tf_op jit(solution)/shard_map/ppermute | solution.py:571
  161.7 25.9 %collective-permute-start.26 = (bf16[256,2048]{1,0:T(8,128)(2,1)}, bf16[256,2048]{1,0:T(8,128)(2,1)}, u32[]{:S(2)}, u32[]{:S(2)}) collective-permute-start(bf16[256,2048]{1,0:T(8,128)(2,1)} %constant_dynamic-update-slice_fusion.24.refs_0_.refs_5_), channel_id=1, source_target_pairs={{0,4},{1,5},{2,6},{3,7},{4,0},{5,1},{6,2},{7,3},{8,12},{9,13},{10,... | collective-permute-start | bytes 3145736 | tf_op jit(solution)/shard_map/ppermute | solution.py:505
  163.0 28.8 %collective-permute-start.27 = (bf16[256,2048]{1,0:T(8,128)(2,1)}, bf16[256,2048]{1,0:T(8,128)(2,1)}, u32[]{:S(2)}, u32[]{:S(2)}) collective-permute-start(bf16[256,2048]{1,0:T(8,128)(2,1)} %constant_dynamic-update-slice_fusion.24.refs_0_.refs_5_), channel_id=1, source_target_pairs={{0,1},{1,0},{2,3},{3,2},{4,5},{5,4},{6,7},{7,6},{8,9},{9,8},{10,11... | collective-permute-start | bytes 3145736 | tf_op jit(solution)/shard_map/ppermute | solution.py:505
  167.7 26.3 %collective-permute-start.21 = (bf16[512,1024]{1,0:T(8,128)(2,1)S(1)}, bf16[512,1024]{1,0:T(8,128)(2,1)S(1)}, u32[]{:S(2)}, u32[]{:S(2)}) collective-permute-start(bf16[512,1024]{1,0:T(8,128)(2,1)S(1)} %get-tuple-element.153), channel_id=1, source_target_pairs={{0,2},{2,0},{1,3},{3,1},{4,6},{6,4},{5,7},{7,5},{8,10},{10,8},{9,1... | collective-permute-start | bytes 3145736 | tf_op jit(solution)/shard_map/ppermute | solution.py:571
  172.4 36.6 %collective-permute-start.36 = (bf16[128,2048]{1,0:T(8,128)(2,1)}, bf16[128,2048]{1,0:T(8,128)(2,1)}, u32[]{:S(2)}, u32[]{:S(2)}) collective-permute-start(bf16[128,2048]{1,0:T(8,128)(2,1)} %slice.330), channel_id=1, source_target_pairs={{0,1},{1,0},{2,3},{3,2},{4,5},{5,4},{6,7},{7,6},{8,9},{9,8},{10,11... | collective-permute-start | bytes 1572872 | tf_op jit(solution)/shard_map/ppermute | solution.py:505
  187.6 21.4 %collective-permute-start.37 = (bf16[128,2048]{1,0:T(8,128)(2,1)}, bf16[128,2048]{1,0:T(8,128)(2,1)}, u32[]{:S(2)}, u32[]{:S(2)}) collective-permute-start(bf16[128,2048]{1,0:T(8,128)(2,1)} %slice.331), channel_id=1, source_target_pairs={{0,4},{1,5},{2,6},{3,7},{4,0},{5,1},{6,2},{7,3},{8,12},{9,13},{10,... | collective-permute-start | bytes 1572872 | tf_op jit(solution)/shard_map/ppermute | solution.py:505
  191.9 47.8 %collective-permute-start.28 = (bf16[128,2048]{1,0:T(8,128)(2,1)}, bf16[128,2048]{1,0:T(8,128)(2,1)}, u32[]{:S(2)}, u32[]{:S(2)}) collective-permute-start(bf16[128,2048]{1,0:T(8,128)(2,1)} %slice.328), channel_id=1, source_target_pairs={{0,1},{1,0},{2,3},{3,2},{4,5},{5,4},{6,7},{7,6},{8,9},{9,8},{10,11... | collective-permute-start | bytes 1572872 | tf_op jit(solution)/shard_map/ppermute | solution.py:505
  195.0 45.5 %collective-permute-start.29 = (bf16[128,2048]{1,0:T(8,128)(2,1)}, bf16[128,2048]{1,0:T(8,128)(2,1)}, u32[]{:S(2)}, u32[]{:S(2)}) collective-permute-start(bf16[128,2048]{1,0:T(8,128)(2,1)} %slice.329), channel_id=1, source_target_pairs={{0,4},{1,5},{2,6},{3,7},{4,0},{5,1},{6,2},{7,3},{8,12},{9,13},{10,... | collective-permute-start | bytes 1572872 | tf_op jit(solution)/shard_map/ppermute | solution.py:505
  234.1 36.0 %collective-permute-start.78 = (bf16[2,128,1024]{2,1,0:T(8,128)(2,1)}, bf16[2,128,1024]{2,1,0:T(8,128)(2,1)S(1)}, u32[]{:S(2)}, u32[]{:S(2)}) collective-permute-start(bf16[2,128,1024]{2,1,0:T(8,128)(2,1)} %get-tuple-element.73), channel_id=1, source_target_pairs={{0,4},{1,5},{2,6},{3,7},{4,0},{5,1},{6,2},{7,3},{8,12},{9,13},{10,... | collective-permute-start | bytes 1572872 | tf_op jit(solution)/shard_map/ppermute | solution.py:505
  235.5 36.7 %collective-permute-start.73 = (bf16[2,128,1024]{2,1,0:T(8,128)(2,1)}, bf16[2,128,1024]{2,1,0:T(8,128)(2,1)S(1)}, u32[]{:S(2)}, u32[]{:S(2)}) collective-permute-start(bf16[2,128,1024]{2,1,0:T(8,128)(2,1)} %get-tuple-element.71), channel_id=1, source_target_pairs={{0,1},{1,0},{2,3},{3,2},{4,5},{5,4},{6,7},{7,6},{8,9},{9,8},{10,11... | collective-permute-start | bytes 1572872 | tf_op jit(solution)/shard_map/ppermute | solution.py:505
  238.3 48.7 %collective-permute-start.75 = (bf16[2,128,1024]{2,1,0:T(8,128)(2,1)S(1)}, bf16[2,128,1024]{2,1,0:T(8,128)(2,1)S(1)}, u32[]{:S(2)}, u32[]{:S(2)}) collective-permute-start(bf16[2,128,1024]{2,1,0:T(8,128)(2,1)S(1)} %slice.294), channel_id=1, source_target_pairs={{0,1},{1,0},{2,3},{3,2},{4,5},{5,4},{6,7},{7,6},{8,9},{9,8},{10,11... | collective-permute-start | bytes 1572872 | tf_op jit(solution)/shard_map/ppermute | solution.py:505
  239.7 48.1 %collective-permute-start.77 = (bf16[2,128,1024]{2,1,0:T(8,128)(2,1)S(1)}, bf16[2,128,1024]{2,1,0:T(8,128)(2,1)}, u32[]{:S(2)}, u32[]{:S(2)}) collective-permute-start(bf16[2,128,1024]{2,1,0:T(8,128)(2,1)S(1)} %slice.298), channel_id=1, source_target_pairs={{0,4},{1,5},{2,6},{3,7},{4,0},{5,1},{6,2},{7,3},{8,12},{9,13},{10,... | collective-permute-start | bytes 1572872 | tf_op jit(solution)/shard_map/ppermute | solution.py:505
  272.2 24.1 %collective-permute-start.79 = (bf16[2,128,1024]{2,1,0:T(8,128)(2,1)S(1)}, bf16[2,128,1024]{2,1,0:T(8,128)(2,1)S(1)}, u32[]{:S(2)}, u32[]{:S(2)}) collective-permute-start(bf16[2,128,1024]{2,1,0:T(8,128)(2,1)S(1)} %add_convert_fusion.8), channel_id=1, source_target_pairs={{0,1},{1,0},{2,3},{3,2},{4,5},{5,4},{6,7},{7,6},{8,9},{9,8},{10,11... | collective-permute-start | bytes 1572872 | tf_op jit(solution)/shard_map/ppermute | solution.py:505
  278.7 19.4 %collective-permute-start.74 = (bf16[2,128,1024]{2,1,0:T(8,128)(2,1)S(1)}, bf16[2,128,1024]{2,1,0:T(8,128)(2,1)S(1)}, u32[]{:S(2)}, u32[]{:S(2)}) collective-permute-start(bf16[2,128,1024]{2,1,0:T(8,128)(2,1)S(1)} %add_convert_fusion.10), channel_id=1, source_target_pairs={{0,4},{1,5},{2,6},{3,7},{4,0},{5,1},{6,2},{7,3},{8,12},{9,13},{10,... | collective-permute-start | bytes 1572872 | tf_op jit(solution)/shard_map/ppermute | solution.py:505
  285.1 22.5 %collective-permute-start.85 = (bf16[2,128,1024]{2,1,0:T(8,128)(2,1)S(1)}, bf16[2,128,1024]{2,1,0:T(8,128)(2,1)S(1)}, u32[]{:S(2)}, u32[]{:S(2)}) collective-permute-start(bf16[2,128,1024]{2,1,0:T(8,128)(2,1)S(1)} %slice.305), channel_id=1, source_target_pairs={{0,1},{1,0},{2,3},{3,2},{4,5},{5,4},{6,7},{7,6},{8,9},{9,8},{10,11... | collective-permute-start | bytes 1572872 | tf_op jit(solution)/shard_map/ppermute | solution.py:505
  287.0 20.5 %collective-permute-start.87 = (bf16[2,128,1024]{2,1,0:T(8,128)(2,1)S(1)}, bf16[2,128,1024]{2,1,0:T(8,128)(2,1)S(1)}, u32[]{:S(2)}, u32[]{:S(2)}) collective-permute-start(bf16[2,128,1024]{2,1,0:T(8,128)(2,1)S(1)} %slice.309), channel_id=1, source_target_pairs={{0,4},{1,5},{2,6},{3,7},{4,0},{5,1},{6,2},{7,3},{8,12},{9,13},{10,... | collective-permute-start | bytes 1572872 | tf_op jit(solution)/shard_map/ppermute | solution.py:505
  287.8 77.5 %collective-permute-start.40 = (bf16[1024,1024]{1,0:T(8,128)(2,1)S(1)}, bf16[1024,1024]{1,0:T(8,128)(2,1)}, u32[]{:S(2)}, u32[]{:S(2)}) collective-permute-start(bf16[1024,1024]{1,0:T(8,128)(2,1)S(1)} %copy-done.2), channel_id=1, source_target_pairs={{0,2},{2,0},{1,3},{3,1},{4,6},{6,4},{5,7},{7,5},{8,10},{10,8},{9,1... | collective-permute-start | bytes 6291464 | tf_op jit(solution)/shard_map/ppermute | solution.py:571
  296.3 19.0 %collective-permute-start.89 = (bf16[2,128,1024]{2,1,0:T(8,128)(2,1)S(1)}, bf16[2,128,1024]{2,1,0:T(8,128)(2,1)S(1)}, u32[]{:S(2)}, u32[]{:S(2)}) collective-permute-start(bf16[2,128,1024]{2,1,0:T(8,128)(2,1)S(1)} %add_convert_fusion.4), channel_id=1, source_target_pairs={{0,1},{1,0},{2,3},{3,2},{4,5},{5,4},{6,7},{7,6},{8,9},{9,8},{10,11... | collective-permute-start | bytes 1572872 | tf_op jit(solution)/shard_map/ppermute | solution.py:505
  298.1 18.4 %collective-permute-start.84 = (bf16[2,128,1024]{2,1,0:T(8,128)(2,1)S(1)}, bf16[2,128,1024]{2,1,0:T(8,128)(2,1)S(1)}, u32[]{:S(2)}, u32[]{:S(2)}) collective-permute-start(bf16[2,128,1024]{2,1,0:T(8,128)(2,1)S(1)} %add_convert_fusion.6), channel_id=1, source_target_pairs={{0,4},{1,5},{2,6},{3,7},{4,0},{5,1},{6,2},{7,3},{8,12},{9,13},{10,... | collective-permute-start | bytes 1572872 | tf_op jit(solution)/shard_map/ppermute | solution.py:505
  307.5 51.0 %collective-permute-start.38 = (bf16[512,1024]{1,0:T(8,128)(2,1)S(1)}, bf16[512,1024]{1,0:T(8,128)(2,1)S(1)}, u32[]{:S(2)}, u32[]{:S(2)}) collective-permute-start(bf16[512,1024]{1,0:T(8,128)(2,1)S(1)} %constant_dynamic-slice_fusion), channel_id=1, source_target_pairs={{0,2},{2,0},{1,3},{3,1},{4,6},{6,4},{5,7},{7,5},{8,10},{10,8},{9,1... | collective-permute-start | bytes 3145736 | tf_op jit(solution)/shard_map/ppermute | solution.py:571
  315.3 28.7 %collective-permute-start.81 = (bf16[2,64,1024]{2,1,0:T(8,128)(2,1)S(1)}, bf16[2,64,1024]{2,1,0:T(8,128)(2,1)S(1)}, u32[]{:S(2)}, u32[]{:S(2)}) collective-permute-start(bf16[2,64,1024]{2,1,0:T(8,128)(2,1)S(1)} %get-tuple-element.107), channel_id=1, source_target_pairs={{0,24},{1,25},{2,26},{3,27},{4,28},{5,29},{6,30},{7,31},{8,16},{9,... | collective-permute-start | bytes 786440 | tf_op jit(solution)/shard_map/ppermute | solution.py:505
  316.5 28.4 %collective-permute-start.76 = (bf16[2,64,1024]{2,1,0:T(8,128)(2,1)S(1)}, bf16[2,64,1024]{2,1,0:T(8,128)(2,1)S(1)}, u32[]{:S(2)}, u32[]{:S(2)}) collective-permute-start(bf16[2,64,1024]{2,1,0:T(8,128)(2,1)S(1)} %slice.364), channel_id=1, source_target_pairs={{0,8},{1,9},{2,10},{3,11},{4,12},{5,13},{6,14},{7,15},{8,0},{9,1},... | collective-permute-start | bytes 786440 | tf_op jit(solution)/shard_map/ppermute | solution.py:505
  325.5 22.5 %collective-permute-start.90 = (bf16[2,64,1024]{2,1,0:T(8,128)(2,1)S(1)}, bf16[2,64,1024]{2,1,0:T(8,128)(2,1)S(1)}, u32[]{:S(2)}, u32[]{:S(2)}) collective-permute-start(bf16[2,64,1024]{2,1,0:T(8,128)(2,1)S(1)} %get-tuple-element.108), channel_id=1, source_target_pairs={{0,16},{1,17},{2,18},{3,19},{4,20},{5,21},{6,22},{7,23},{8,24},{9,... | collective-permute-start | bytes 786440 | tf_op jit(solution)/shard_map/ppermute | solution.py:505
  361.1 85.1 %collective-permute-start.39 = (bf16[512,1024]{1,0:T(8,128)(2,1)}, bf16[512,1024]{1,0:T(8,128)(2,1)}, u32[]{:S(2)}, u32[]{:S(2)}) collective-permute-start(bf16[512,1024]{1,0:T(8,128)(2,1)} %fusion.25), channel_id=1, source_target_pairs={{0,0},{2,1},{1,2},{3,3},{4,4},{6,5},{5,6},{7,7},{8,8},{10,9},{9,10... | collective-permute-start | bytes 3145736 | tf_op jit(solution)/shard_map/ppermute | solution.py:497
  380.4 32.7 %collective-permute-start.68 = (f32[8192]{0:T(1024)S(1)}, f32[8192]{0:T(1024)S(1)}, u32[]{:S(2)}, u32[]{:S(2)}) collective-permute-start(f32[8192]{0:T(1024)S(1)} %pad_maximum_fusion.6), channel_id=1, source_target_pairs={{0,4},{1,5},{2,6},{3,7},{4,0},{5,1},{6,2},{7,3},{8,12},{9,13},{10,... | collective-permute-start | bytes 98312 | tf_op jit(solution)/shard_map/ppermute | solution.py:505
  421.2 21.7 %collective-permute-start.63 = (bf16[1,128,512]{2,1,0:T(8,128)(2,1)}, bf16[1,128,512]{2,1,0:T(8,128)(2,1)S(1)}, u32[]{:S(2)}, u32[]{:S(2)}) collective-permute-start(bf16[1,128,512]{2,1,0:T(8,128)(2,1)} %get-tuple-element.96), channel_id=1, source_target_pairs={{0,4},{1,5},{2,6},{3,7},{4,0},{5,1},{6,2},{7,3},{8,12},{9,13},{10,... | collective-permute-start | bytes 393224 | tf_op jit(solution)/shard_map/ppermute | solution.py:505
  422.5 22.0 %collective-permute-start.58 = (bf16[1,128,512]{2,1,0:T(8,128)(2,1)}, bf16[1,128,512]{2,1,0:T(8,128)(2,1)}, u32[]{:S(2)}, u32[]{:S(2)}) collective-permute-start(bf16[1,128,512]{2,1,0:T(8,128)(2,1)} %get-tuple-element.95), channel_id=1, source_target_pairs={{0,1},{1,0},{2,3},{3,2},{4,5},{5,4},{6,7},{7,6},{8,9},{9,8},{10,11... | collective-permute-start | bytes 393224 | tf_op jit(solution)/shard_map/ppermute | solution.py:505
  429.6 24.3 %collective-permute-start.60 = (bf16[1,128,512]{2,1,0:T(8,128)(2,1)}, bf16[1,128,512]{2,1,0:T(8,128)(2,1)}, u32[]{:S(2)}, u32[]{:S(2)}) collective-permute-start(bf16[1,128,512]{2,1,0:T(8,128)(2,1)} %slice.351), channel_id=1, source_target_pairs={{0,1},{1,0},{2,3},{3,2},{4,5},{5,4},{6,7},{7,6},{8,9},{9,8},{10,11... | collective-permute-start | bytes 393224 | tf_op jit(solution)/shard_map/ppermute | solution.py:505
  456.0 18.6 %collective-permute-start.50 = (bf16[3,128,512]{2,1,0:T(8,128)(2,1)}, bf16[3,128,512]{2,1,0:T(8,128)(2,1)S(1)}, u32[]{:S(2)}, u32[]{:S(2)}) collective-permute-start(bf16[3,128,512]{2,1,0:T(8,128)(2,1)} %slice.260), channel_id=1, source_target_pairs={{0,1},{1,0},{2,3},{3,2},{4,5},{5,4},{6,7},{7,6},{8,9},{9,8},{10,11... | collective-permute-start | bytes 1179656 | tf_op jit(solution)/shard_map/ppermute | solution.py:505
  456.0 30.7 %collective-permute-start.41 = (bf16[512,1024]{1,0:T(8,128)(2,1)}, bf16[512,1024]{1,0:T(8,128)(2,1)S(1)}, u32[]{:S(2)}, u32[]{:S(2)}) collective-permute-start(bf16[512,1024]{1,0:T(8,128)(2,1)} %constant_dynamic-slice_fusion.1), channel_id=1, source_target_pairs={{0,2},{2,0},{1,3},{3,1},{4,6},{6,4},{5,7},{7,5},{8,10},{10,8},{9,1... | collective-permute-start | bytes 3145736 | tf_op jit(solution)/shard_map/ppermute | solution.py:571
  474.6 39.0 %collective-permute-start.67 = (bf16[1,64,512]{2,1,0:T(8,128)(2,1)}, bf16[1,64,512]{2,1,0:T(8,128)(2,1)}, u32[]{:S(2)}, u32[]{:S(2)}) collective-permute-start(bf16[1,64,512]{2,1,0:T(8,128)(2,1)} %add_convert_fusion.22), channel_id=1, source_target_pairs={{0,0},{2,1},{1,2},{3,3},{4,4},{6,5},{5,6},{7,7},{8,8},{10,9},{9,10... | collective-permute-start | bytes 196616 | tf_op jit(solution)/shard_map/ppermute | solution.py:497
  504.8 30.4 %collective-permute-start.42 = (bf16[512,1024]{1,0:T(8,128)(2,1)S(1)}, bf16[512,1024]{1,0:T(8,128)(2,1)S(1)}, u32[]{:S(2)}, u32[]{:S(2)}) collective-permute-start(bf16[512,1024]{1,0:T(8,128)(2,1)S(1)} %fusion.26), channel_id=1, source_target_pairs={{0,0},{2,1},{1,2},{3,3},{4,4},{6,5},{5,6},{7,7},{8,8},{10,9},{9,10... | collective-permute-start | bytes 3145736 | tf_op jit(solution)/shard_map/ppermute | solution.py:497
  (94 other events, 2597.7 us)
